TPU v7x, 512 devices: a whole 4x4x16 slice. The times are simulated.
512 devices in a mesh: blk: 128 (over z_lo, x, y), red: 4 (over z_hi, core).
Axes of the slice: x: 4, y: 4, z: 16 (z_hi: 2, z_lo: 8; z = z_hi * 8 + z_lo), core: 2. Of those that a mesh axis runs over, the one named last changes fastest.
Arguments:
- amplitudes: bfloat16 [8192, 16384], P('blk', 'red'), may hold values from -6 to 6
- integrals: bfloat16 [65536, 16384], P('blk', 'red'), may hold values from -0.046875 to 0.046875
- occ_live: int32 [8], replicated, may hold values from 256 to 1024, as said below
Outputs:
- residual: bfloat16 [1024, 65536], P('red', 'blk')
Inputs may be any that keep to these rules, and one draw needn't show every extreme that they name: Rows ij at or past occ_live[s] of sector s are padding; some sector is always full, with 1024 live pairs.
All inputs are finite; a program needn't handle non-finite values.
Results may differ from a plain program's by a relative error of at most 0.001.
Values may be sent and summed in bfloat16 or wider, within the bound.
No kernel may reach another device: no remote copies, remote signals or barrier semaphores. Data moves between devices by JAX's collectives and lax.ppermute only.
A program may use at most 128 MiB of HBM per device.

v0:
```python
import jax
import jax.numpy as jnp
from jax import lax
from jax.sharding import PartitionSpec as P


def partner(block, axis, stride):
    count = lax.axis_size(axis)
    route = []
    for low in range(count):
        high = low | 1 << stride
        if high != low and high < count:
            route += [(low, high), (high, low)]
    return lax.ppermute(block, axis, route)


def select_entry(table, position):
    places = jnp.arange(table.shape[0], dtype=jnp.int32)
    return jnp.sum(jnp.where(places == position, table, jnp.zeros((), table.dtype)))


def collect(amplitudes, member, levels, visit, state):
    held = amplitudes
    ij_dev = amplitudes.shape[0]
    for bit in range(levels):
        other = partner(held, "blk", bit)
        span = ij_dev << bit
        other_start = (member >> bit ^ 1) * span
        state = visit(state, other, other_start)
        upper = member >> bit & 1 == 1
        held = jnp.where(
            upper, jnp.concatenate([other, held], 0), jnp.concatenate([held, other], 0)
        )
    return (held, state)


def on_device(amplitudes, integrals, occ_live):
    ij_dev = amplitudes.shape[0]
    ab_dev = integrals.shape[0]
    group = min(16, lax.axis_size("blk") // 2)
    levels = group.bit_length() - 1
    index = lax.axis_index("blk")
    sector = index // group
    member = index % group
    live = select_entry(occ_live, sector)
    ij_sec = ij_dev * group
    rows_red = ij_sec // lax.axis_size("red")

    def product(piece):
        return lax.dot_general(
            piece, integrals, (((1,), (1,)), ((), ())), preferred_element_type=jnp.float32
        )

    def guarded(piece):
        return product(piece)

    def place(partial_value, piece, start):
        return lax.dynamic_update_slice_in_dim(partial_value, guarded(piece), start, 0)

    own_start = member * ij_dev
    partial_value = place(jnp.zeros((ij_sec, ab_dev), jnp.float32), amplitudes, own_start)
    held, partial_value = collect(amplitudes, member, levels, place, partial_value)
    summed = lax.psum_scatter(partial_value, "red", scatter_dimension=0, tiled=True)
    my_rows = lax.axis_index("red") * rows_red + jnp.arange(rows_red, dtype=jnp.int32)
    kept = jnp.where((my_rows < live)[:, None], summed, jnp.zeros((), jnp.float32))
    return kept.astype(jnp.bfloat16)


def solution(mesh):
    in_specs = (P("blk", "red"), P("blk", "red"), P())
    out_specs = P("red", "blk")
    return jax.shard_map(
        on_device, mesh=mesh, in_specs=in_specs, out_specs=out_specs, check_vma=False
    )
```

profile of v0, /device:TPU:1, one launch (start us, length us, event | category | flops | bytes accessed | tf_op | source)
XLA Modules:
  0.0 314.9 jit_solution(1029106830945975931)
XLA Ops:
  6.5 0.0 reduce-scatter.2.cloned.1.call-start
  6.5 4.0 %collective-permute-start = (bf16[64,4096]{1,0:T(8,128)(2,1)}, bf16[64,4096]{1,0:T(8,128)(2,1)S(1)}, u32[]{:S(2)}, u32[]{:S(2)}) collective-permute-start(bf16[64,4096]{1,0:T(8,128)(2,1)} %param.3), channel_id=1, source_target_pairs={{0,4},{4,0},{8,12},{12,8},{16,20},{20,16},{24,28},{28,24},{32,36},... | collective-permute-start | bytes 1572872 | tf_op jit(solution)/shard_map/ppermute | solution.py:14
  10.6 7.0 %collective-permute-done = bf16[64,4096]{1,0:T(8,128)(2,1)S(1)} collective-permute-done((bf16[64,4096]{1,0:T(8,128)(2,1)}, bf16[64,4096]{1,0:T(8,128)(2,1)S(1)}, u32[]{:S(2)}, u32[]{:S(2)}) %collective-permute-start) | collective-permute-done | bytes 524320 | tf_op jit(solution)/shard_map/ppermute | solution.py:14
  17.6 1.6 maximum_select_fusion.2
  19.2 9.5 %collective-permute-start.1 = (bf16[128,4096]{1,0:T(8,128)(2,1)S(1)}, bf16[128,4096]{1,0:T(8,128)(2,1)}, u32[]{:S(2)}, u32[]{:S(2)}) collective-permute-start(bf16[128,4096]{1,0:T(8,128)(2,1)S(1)} %maximum_select_fusion.2), channel_id=1, source_target_pairs={{0,8},{8,0},{4,12},{12,4},{16,24},{24,16},{20,28},{28,20},{32,40},... | collective-permute-start | bytes 3145736 | tf_op jit(solution)/shard_map/ppermute | solution.py:14
  28.7 0.0 copy-done.3
  28.7 20.9 %collective-permute-done.1 = bf16[128,4096]{1,0:T(8,128)(2,1)} collective-permute-done((bf16[128,4096]{1,0:T(8,128)(2,1)S(1)}, bf16[128,4096]{1,0:T(8,128)(2,1)}, u32[]{:S(2)}, u32[]{:S(2)}) %collective-permute-start.1) | collective-permute-done | bytes 1048608 | tf_op jit(solution)/shard_map/ppermute | solution.py:14
  49.6 2.2 maximum_select_fusion.1
  51.8 4.0 %collective-permute-start.2 = (bf16[256,4096]{1,0:T(8,128)(2,1)S(1)}, bf16[256,4096]{1,0:T(8,128)(2,1)}, u32[]{:S(2)}, u32[]{:S(2)}) collective-permute-start(bf16[256,4096]{1,0:T(8,128)(2,1)S(1)} %maximum_select_fusion.1), channel_id=1, source_target_pairs={{0,16},{16,0},{4,20},{20,4},{8,24},{24,8},{12,28},{28,12},{32,48},... | collective-permute-start | bytes 6291464 | tf_op jit(solution)/shard_map/ppermute | solution.py:14
  55.9 0.0 copy-start.2
  55.9 43.1 %collective-permute-done.2 = bf16[256,4096]{1,0:T(8,128)(2,1)} collective-permute-done((bf16[256,4096]{1,0:T(8,128)(2,1)S(1)}, bf16[256,4096]{1,0:T(8,128)(2,1)}, u32[]{:S(2)}, u32[]{:S(2)}) %collective-permute-start.2) | collective-permute-done | bytes 2097184 | tf_op jit(solution)/shard_map/ppermute | solution.py:14
  98.9 4.7 %maximum_select_fusion = bf16[512,4096]{1,0:T(8,128)(2,1)} fusion(bf16[256,4096]{1,0:T(8,128)(2,1)S(1)} %maximum_select_fusion.1, bf16[256,4096]{1,0:T(8,128)(2,1)} %collective-permute-done.2, pred[]{:T(512)S(6)} %eq.21), kind=kLoop, calls=%fused_computation | loop fusion | flops 18874368 | bytes 8388609 | tf_op jit(solution)/shard_map/jit(_where)/select_n | solution.py:31
  103.6 5.2 %collective-permute-start.3 = (bf16[512,4096]{1,0:T(8,128)(2,1)}, bf16[512,4096]{1,0:T(8,128)(2,1)}, u32[]{:S(2)}, u32[]{:S(2)}) collective-permute-start(bf16[512,4096]{1,0:T(8,128)(2,1)} %maximum_select_fusion), channel_id=1, source_target_pairs={{0,32},{32,0},{4,36},{36,4},{8,40},{40,8},{12,44},{44,12},{16,48},... | collective-permute-start | bytes 12582920 | tf_op jit(solution)/shard_map/ppermute | solution.py:14
  108.9 0.0 copy-start
  108.9 0.2 broadcast_in_dim.22
  109.2 0.0 copy-done.2
  109.2 3.7 %convolution_dynamic-update-slice_fusion.4 = f32[1024,512]{1,0:T(8,128)S(1)} fusion(f32[1024,512]{1,0:T(8,128)S(1)} %broadcast_in_dim.22, s32[]{:T(128)S(6)} %select_n.61, bf16[64,4096]{1,0:T(8,128)(2,1)S(1)} %copy-done.2, bf16[512,4096]{1,0:T(8,128)(2,1)} %param.4), kind=kOutput, calls=%fused_computation.6 | convolution fusion | flops 268435456 | bytes 4849668 | tf_op jit(solution)/shard_map/dot_general | solution.py:50
  112.9 0.0 copy-done.4
  112.9 0.0 copy-done
  112.9 1.4 convolution_dynamic-update-slice_fusion.3
  114.3 2.8 convolution_dynamic-update-slice_fusion.2
  117.1 2.9 convolution_dynamic-update-slice_fusion.1
  120.0 0.0 copy-start.5
  120.0 76.4 %collective-permute-done.3 = bf16[512,4096]{1,0:T(8,128)(2,1)} collective-permute-done((bf16[512,4096]{1,0:T(8,128)(2,1)}, bf16[512,4096]{1,0:T(8,128)(2,1)}, u32[]{:S(2)}, u32[]{:S(2)}) %collective-permute-start.3) | collective-permute-done | bytes 4194336 | tf_op jit(solution)/shard_map/ppermute | solution.py:14
  196.4 4.5 %convolution_dynamic-update-slice_fusion = f32[1024,512]{1,0:T(8,128)S(1)} fusion(f32[1024,512]{1,0:T(8,128)S(1)} %convolution_dynamic-update-slice_fusion.1, s32[]{:T(128)S(6)} %select_n.71, bf16[512,4096]{1,0:T(8,128)(2,1)} %collective-permute-done.3, bf16[512,4096]{1,0:T(8,128)(2,1)S(1)} %copy-done), kind=kOutput, calls=%fused_computation.2 | convolution fusion | flops 2147483648 | bytes 9437188 | tf_op jit(solution)/shard_map/dot_general | solution.py:50
  201.0 0.0 copy-start.1
  201.0 1.3 copy-done.1
  202.3 0.0 reduce-scatter.2.cloned.1.call-update
  202.4 0.6 fusion
  203.0 0.7 add_compare_fusion
  203.6 102.6 %reduce-scatter.2.cloned.1.call-done = f32[256,512]{1,0:T(8,128)} async-done(((f32[1024,512]{1,0:T(8,128)}), f32[256,512]{1,0:T(8,128)}) %reduce-scatter.2.cloned.1.call-update) | async-done | bytes 524304 | tf_op jit(solution)/shard_map/reduce_scatter | solution.py:63
  306.2 1.8 select_convert_fusion
  (3 shorter events, 0.0 us)
Async XLA Ops:
  6.5 299.7 %reduce-scatter.2.cloned.1.call-start = ((), (), s32[]{:S(2)}) async-start(), calls=%async_computation.1 | async-start | bytes 2621440 | tf_op jit(solution)/shard_map/reduce_scatter | solution.py:63
  6.5 11.1 %collective-permute-start = (bf16[64,4096]{1,0:T(8,128)(2,1)}, bf16[64,4096]{1,0:T(8,128)(2,1)S(1)}, u32[]{:S(2)}, u32[]{:S(2)}) collective-permute-start(bf16[64,4096]{1,0:T(8,128)(2,1)} %param.3), channel_id=1, source_target_pairs={{0,4},{4,0},{8,12},{12,8},{16,20},{20,16},{24,28},{28,24},{32,36},... | collective-permute-start | bytes 1572872 | tf_op jit(solution)/shard_map/ppermute | solution.py:14
  17.6 11.1 %copy-start.3 = (bf16[64,4096]{1,0:T(8,128)(2,1)}, bf16[64,4096]{1,0:T(8,128)(2,1)S(1)}, u32[]{:S(2)}) copy-start(bf16[64,4096]{1,0:T(8,128)(2,1)S(1)} %collective-permute-done) | copy-start | bytes 1572868
  19.2 30.4 %collective-permute-start.1 = (bf16[128,4096]{1,0:T(8,128)(2,1)S(1)}, bf16[128,4096]{1,0:T(8,128)(2,1)}, u32[]{:S(2)}, u32[]{:S(2)}) collective-permute-start(bf16[128,4096]{1,0:T(8,128)(2,1)S(1)} %maximum_select_fusion.2), channel_id=1, source_target_pairs={{0,8},{8,0},{4,12},{12,4},{16,24},{24,16},{20,28},{28,20},{32,40},... | collective-permute-start | bytes 3145736 | tf_op jit(solution)/shard_map/ppermute | solution.py:14
  51.8 47.1 %collective-permute-start.2 = (bf16[256,4096]{1,0:T(8,128)(2,1)S(1)}, bf16[256,4096]{1,0:T(8,128)(2,1)}, u32[]{:S(2)}, u32[]{:S(2)}) collective-permute-start(bf16[256,4096]{1,0:T(8,128)(2,1)S(1)} %maximum_select_fusion.1), channel_id=1, source_target_pairs={{0,16},{16,0},{4,20},{20,4},{8,24},{24,8},{12,28},{28,12},{32,48},... | collective-permute-start | bytes 6291464 | tf_op jit(solution)/shard_map/ppermute | solution.py:14
  55.9 53.3 %copy-start.2 = (bf16[64,4096]{1,0:T(8,128)(2,1)S(1)}, bf16[64,4096]{1,0:T(8,128)(2,1)}, u32[]{:S(2)}) copy-start(bf16[64,4096]{1,0:T(8,128)(2,1)} %param.3) | copy-start | bytes 1572868
  103.6 9.3 %copy-start.4 = (bf16[64,4096]{1,0:T(8,128)(2,1)S(1)}, bf16[64,4096]{1,0:T(8,128)(2,1)}, u32[]{:S(2)}) copy-start(bf16[64,4096]{1,0:T(8,128)(2,1)} %copy-done.3) | copy-start | bytes 1572868
  103.6 92.8 %collective-permute-start.3 = (bf16[512,4096]{1,0:T(8,128)(2,1)}, bf16[512,4096]{1,0:T(8,128)(2,1)}, u32[]{:S(2)}, u32[]{:S(2)}) collective-permute-start(bf16[512,4096]{1,0:T(8,128)(2,1)} %maximum_select_fusion), channel_id=1, source_target_pairs={{0,32},{32,0},{4,36},{36,4},{8,40},{40,8},{12,44},{44,12},{16,48},... | collective-permute-start | bytes 12582920 | tf_op jit(solution)/shard_map/ppermute | solution.py:14
  108.9 4.0 %copy-start = (bf16[512,4096]{1,0:T(8,128)(2,1)S(1)}, bf16[512,4096]{1,0:T(8,128)(2,1)}, u32[]{:S(2)}) copy-start(bf16[512,4096]{1,0:T(8,128)(2,1)} %param.4) | copy-start | bytes 12582916
  120.0 82.4 %copy-start.5 = (s32[8]{0:T(128)S(1)}, s32[8]{0:T(128)}, u32[]{:S(2)}) copy-start(s32[8]{0:T(128)} %param.5) | copy-start | bytes 100
  201.0 1.3 copy-start.1
Sparse Core Ops, SparseCore 0:
  202.4 103.7 reduce-scatter.1
where the time goes:
time: 315 us
  waiting for transfers between devices  250 us (79%)
  starting transfers between devices  22.7 us (7%)
  matrix products  15.3 us (5%)
  between operations  13.6 us (4%)
  other arithmetic  11.7 us (4%)
    ppermute x4, waiting for transfers between devices, partner(): return lax.ppermute(block, axis, route)  147 us
    reduce_scatter x1, waiting for transfers between devices, on_device(): lax.psum_scatter(partial_value, 'red', scatter_dimension=0, tiled=True)  103 us
    ppermute x4, starting transfers between devices, partner(): return lax.ppermute(block, axis, route)  22.7 us
    dot_general x5, matrix products, product(): lax.dot_general(piece, integrals, (((1,), (1,)), ((), ())), preferred_ele...  15.3 us
    select_n x3, other arithmetic, collect(): jnp.where(upper, jnp.concatenate([other, held], 0), jnp.concatenate([held...  8.54 us
  transfers between devices with their start and end apart: 5, of which 5 were waited for; matrix products, arithmetic and copies ran while one was open for 4% of the time, Pallas kernels for 0%

commit v1 on v0

v1 whole, which is shorter than its diff:
```python
import jax
import jax.numpy as jnp
from jax import lax
from jax.sharding import PartitionSpec as P

LANES = 128


def power_steps():
    return [(float(2**j), 2.0 ** (2**j), 2.0 ** -(2**j)) for j in (6, 5, 4, 3, 2, 1)]


def scaled_rows(block):
    wide = block.astype(jnp.float32)
    largest = jnp.max(jnp.abs(wide), axis=1, keepdims=True)
    scale = jnp.ones_like(largest)
    exponent = jnp.zeros_like(largest)
    for step, up, _ in power_steps():
        fits = largest * scale * up <= 32768.0
        scale = jnp.where(fits, scale * up, scale)
        exponent = jnp.where(fits, exponent + step, exponent)
    rows = (wide * scale).astype(jnp.float16)
    tail = jnp.broadcast_to(exponent, (block.shape[0], LANES)).astype(jnp.float16)
    return jnp.concatenate([rows, tail], 1)


def unscale(exponent):
    left = exponent.astype(jnp.float32)
    factor = jnp.ones_like(left)
    for step, _, down in power_steps():
        taken = left >= step
        factor = jnp.where(taken, factor * down, factor)
        left = jnp.where(taken, left - step, left)
    return factor


def on_device(amplitudes, integrals, occ_live):
    ij_dev, cd_dev = amplitudes.shape
    n_blk, n_red = lax.axis_size("blk"), lax.axis_size("red")
    group = 16
    planes = [[s * group + m for m in range(group)] for s in range(n_blk // group)]
    ij_sec = ij_dev * group
    rows_red = ij_sec // n_red
    half = ij_sec // 2
    red = lax.axis_index("red")
    z_half, core = red // 2, red % 2
    sector = lax.axis_index("blk") // group
    live = jnp.sum(jnp.where(jnp.arange(occ_live.shape[0]) == sector, occ_live, 0))

    gathered = lax.all_gather(
        scaled_rows(amplitudes), "blk", axis_index_groups=planes, axis=0, tiled=True
    )

    def partial_rows(start):
        rows = lax.dynamic_slice_in_dim(gathered, start, half, 0)
        product = lax.dot_general(
            rows[:, :cd_dev].astype(jnp.bfloat16),
            integrals,
            (((1,), (1,)), ((), ())),
            preferred_element_type=jnp.float32,
        )
        product = product * unscale(rows[:, cd_dev : cd_dev + 1])
        return product.reshape(2, rows_red, product.shape[1])

    def core_sum(parts):
        mine = jnp.where(core == 0, parts[0], parts[1])
        other = jnp.where(core == 0, parts[1], parts[0])
        got = lax.ppermute(other, "red", [(r, r ^ 1) for r in range(n_red)])
        return mine + got

    away = core_sum(partial_rows((1 - z_half) * half))
    came = lax.ppermute(away, "red", [(r, r ^ 2) for r in range(n_red)])
    summed = core_sum(partial_rows(z_half * half)) + came
    my_rows = red * rows_red + jnp.arange(rows_red, dtype=jnp.int32)
    kept = jnp.where((my_rows < live)[:, None], summed, jnp.zeros((), jnp.float32))
    return kept.astype(jnp.bfloat16)


def solution(mesh):
    in_specs = (P("blk", "red"), P("blk", "red"), P())
    out_specs = P("red", "blk")
    return jax.shard_map(
        on_device, mesh=mesh, in_specs=in_specs, out_specs=out_specs, check_vma=False
    )
```

time: 315 us -> 136 us (0.43)
  the two profiles are of different devices: /device:TPU:1 before, /device:TPU:32 now
where the time goes in v1:
time: 136 us; the launch traced here: 135 us
  blocking collectives  53.8 us (40%)
  waiting for transfers between devices  44.8 us (33%)
  starting transfers between devices  19.2 us (14%)
  matrix products  10.7 us (8%)
  other arithmetic  6.61 us (5%)
    all_gather x1, blocking collectives, on_device(): lax.all_gather(scaled_rows(amplitudes), 'blk', axis_index_groups=planes,...  53.8 us
    ppermute x1, waiting for transfers between devices, on_device(): came = lax.ppermute(away, 'red', [(r, r ^ 2) for r in range(n_red)])  44.8 us
    ppermute x1, starting transfers between devices, on_device(): came = lax.ppermute(away, 'red', [(r, r ^ 2) for r in range(n_red)])  14.8 us
    dot_general x2, matrix products, partial_rows(): lax.dot_general(rows[:, :cd_dev].astype(jnp.bfloat16), integrals, (((1,),...  10.7 us
    ppermute x2, starting transfers between devices, core_sum(): got = lax.ppermute(other, 'red', [(r, r ^ 1) for r in range(n_red)])  4.33 us
  transfers between devices with their start and end apart: 3, of which 1 were waited for; matrix products, arithmetic and copies ran while one was open for 5% of the time, Pallas kernels for 0%

profile of v1, /device:TPU:32, one launch (start us, length us, event | category | flops | bytes accessed | tf_op | source)
XLA Modules:
  0.0 135.3 jit_solution(4164756721278099077)
XLA Ops:
  0.0 1.2 fusion.4
  1.3 1.2 fusion.5
  2.5 0.1 broadcast_in_dim.33
  2.6 0.1 pad_maximum_fusion
  2.7 53.8 %all-gather.1 = f16[1024,4224]{1,0:T(8,128)(2,1)} all-gather(f16[64,4224]{1,0:T(8,128)(2,1)S(1)} %pad_maximum_fusion), channel_id=1, replica_groups={{0,4,8,12,16,20,24,28,32,36,40,44,48,52,56,60},{64,68,72,76,80,84,88,92..., dimensions={0}, use_global_device_ids=true | all-gather | bytes 9191424 | tf_op jit(solution)/shard_map/all_gather | solution.py:50
  56.5 1.6 %fusion.8 = (f32[512]{0:T(512)S(1)}, f32[512]{0:T(512)S(1)}) fusion(f16[1024,4224]{1,0:T(8,128)(2,1)} %all-gather.1, s32[]{:T(128)S(6)} %select_n.244, s32[]{:T(128)S(6)} %add.112, s32[]{:T(128)S(6)} %select_n.258), kind=kLoop, calls=%fused_computation.39 | loop fusion | flops 28672 | bytes 6156 | tf_op jit(solution)/shard_map/jit(_where)/select_n | solution.py:32
  58.1 0.0 copy-start
  58.1 6.0 %fusion.3 = f32[512,512]{1,0:T(8,128)S(1)} fusion(bf16[512,4096]{1,0:T(8,128)(2,1)} %param.4, f16[1024,4224]{1,0:T(8,128)(2,1)} %all-gather.1, s32[]{:T(128)S(6)} %select_n.258, f32[512]{0:T(512)S(1)} %get-tuple-element.6), kind=kOutput, calls=%fused_computation.5 | convolution fusion | flops 2149842944 | bytes 9439236 | tf_op jit(solution)/shard_map/dot_general | solution.py:56
  64.1 0.1 slice_select_fusion
  64.2 1.9 %collective-permute-start.1 = (f32[256,512]{1,0:T(8,128)S(1)}, f32[256,512]{1,0:T(8,128)S(1)}, u32[]{:S(2)}, u32[]{:S(2)}) collective-permute-start(f32[256,512]{1,0:T(8,128)S(1)} %slice_select_fusion), channel_id=1, source_target_pairs={{0,1},{1,0},{2,3},{3,2},{4,5},{5,4},{6,7},{7,6},{8,9},{9,8},{10,11... | collective-permute-start | bytes 1572872 | tf_op jit(solution)/shard_map/ppermute | solution.py:68
  66.1 0.0 copy-done
  66.1 0.0 copy-start.1
  66.1 4.7 %fusion.2 = f32[512,512]{1,0:T(8,128)S(1)} fusion(bf16[512,4096]{1,0:T(8,128)(2,1)S(1)} %copy-done, f16[1024,4224]{1,0:T(8,128)(2,1)} %all-gather.1, s32[]{:T(128)S(6)} %select_n.244, f32[512]{0:T(512)S(1)} %get-tuple-element.5), kind=kOutput, calls=%fused_computation.4 | convolution fusion | flops 2149842944 | bytes 9439236 | tf_op jit(solution)/shard_map/dot_general | solution.py:56
  70.8 0.1 slice_select_fusion.1
  70.9 2.4 %collective-permute-start = (f32[256,512]{1,0:T(8,128)S(1)}, f32[256,512]{1,0:T(8,128)S(1)}, u32[]{:S(2)}, u32[]{:S(2)}) collective-permute-start(f32[256,512]{1,0:T(8,128)S(1)} %slice_select_fusion.1), channel_id=1, source_target_pairs={{0,1},{1,0},{2,3},{3,2},{4,5},{5,4},{6,7},{7,6},{8,9},{9,8},{10,11... | collective-permute-start | bytes 1572872 | tf_op jit(solution)/shard_map/ppermute | solution.py:68
  73.3 0.0 collective-permute-done.1
  73.3 0.1 select_add_fusion
  73.5 14.8 %collective-permute-start.2 = (f32[256,512]{1,0:T(8,128)S(1)}, f32[256,512]{1,0:T(8,128)S(1)}, u32[]{:S(2)}, u32[]{:S(2)}) collective-permute-start(f32[256,512]{1,0:T(8,128)S(1)} %select_add_fusion), channel_id=1, source_target_pairs={{0,2},{1,3},{2,0},{3,1},{4,6},{5,7},{6,4},{7,5},{8,10},{9,11},{10,... | collective-permute-start | bytes 1572872 | tf_op jit(solution)/shard_map/ppermute | solution.py:72
  88.3 0.0 copy-done.1
  88.4 0.6 fusion.10
  89.0 0.7 add_compare_fusion
  89.6 0.0 collective-permute-done
  89.7 44.8 %collective-permute-done.2 = f32[256,512]{1,0:T(8,128)S(1)} collective-permute-done((f32[256,512]{1,0:T(8,128)S(1)}, f32[256,512]{1,0:T(8,128)S(1)}, u32[]{:S(2)}, u32[]{:S(2)}) %collective-permute-start.2) | collective-permute-done | bytes 524320 | tf_op jit(solution)/shard_map/ppermute | solution.py:72
  134.5 0.8 select_convert_fusion
  (2 shorter events, 0.0 us)
Async XLA Ops:
  58.1 8.0 %copy-start = (bf16[512,4096]{1,0:T(8,128)(2,1)S(1)}, bf16[512,4096]{1,0:T(8,128)(2,1)}, u32[]{:S(2)}) copy-start(bf16[512,4096]{1,0:T(8,128)(2,1)} %param.4) | copy-start | bytes 12582916
  64.2 9.2 %collective-permute-start.1 = (f32[256,512]{1,0:T(8,128)S(1)}, f32[256,512]{1,0:T(8,128)S(1)}, u32[]{:S(2)}, u32[]{:S(2)}) collective-permute-start(f32[256,512]{1,0:T(8,128)S(1)} %slice_select_fusion), channel_id=1, source_target_pairs={{0,1},{1,0},{2,3},{3,2},{4,5},{5,4},{6,7},{7,6},{8,9},{9,8},{10,11... | collective-permute-start | bytes 1572872 | tf_op jit(solution)/shard_map/ppermute | solution.py:68
  66.1 22.3 %copy-start.1 = (s32[8]{0:T(128)S(1)}, s32[8]{0:T(128)}, u32[]{:S(2)}) copy-start(s32[8]{0:T(128)} %param.5) | copy-start | bytes 100
  70.9 18.7 %collective-permute-start = (f32[256,512]{1,0:T(8,128)S(1)}, f32[256,512]{1,0:T(8,128)S(1)}, u32[]{:S(2)}, u32[]{:S(2)}) collective-permute-start(f32[256,512]{1,0:T(8,128)S(1)} %slice_select_fusion.1), channel_id=1, source_target_pairs={{0,1},{1,0},{2,3},{3,2},{4,5},{5,4},{6,7},{7,6},{8,9},{9,8},{10,11... | collective-permute-start | bytes 1572872 | tf_op jit(solution)/shard_map/ppermute | solution.py:68
  73.5 61.0 %collective-permute-start.2 = (f32[256,512]{1,0:T(8,128)S(1)}, f32[256,512]{1,0:T(8,128)S(1)}, u32[]{:S(2)}, u32[]{:S(2)}) collective-permute-start(f32[256,512]{1,0:T(8,128)S(1)} %select_add_fusion), channel_id=1, source_target_pairs={{0,2},{1,3},{2,0},{3,1},{4,6},{5,7},{6,4},{7,5},{8,10},{9,11},{10,... | collective-permute-start | bytes 1572872 | tf_op jit(solution)/shard_map/ppermute | solution.py:72

commit v2 on v0

v2 whole, which is shorter than its diff:
```python
import jax
import jax.numpy as jnp
from jax import lax
from jax.sharding import PartitionSpec as P

GROUP = 16
AXES = ("blk", "red")


def halves(block):
    middle = block.shape[0] // 2
    return block[:middle], block[middle:]


def join(*blocks):
    return jnp.concatenate(blocks, 0)


def hop(block, mask_first, mask_second):
    n_blk, n_red = lax.axis_size("blk"), lax.axis_size("red")
    route = []
    for b in range(n_blk):
        for r in range(n_red):
            route.append((b * n_red + r, (b ^ (mask_second if r % 2 else mask_first)) * n_red + r))
    return lax.ppermute(block, AXES, route)


def between_cores(block):
    return lax.ppermute(block, "red", [(r, r ^ 1) for r in range(lax.axis_size("red"))])


def between_planes(block, sends):
    n_blk, n_red = lax.axis_size("blk"), lax.axis_size("red")
    route = []
    for b in range(n_blk):
        for r in range(n_red):
            early = (b % GROUP) // 8 != r // 2
            if sends(r % 2, early):
                route.append((b * n_red + r, b * n_red + (r ^ 2)))
    return lax.ppermute(block, AXES, route)


def on_device(amplitudes, integrals, occ_live):
    ij_dev, cd_dev = amplitudes.shape
    blk, red = lax.axis_index("blk"), lax.axis_index("red")
    first = red % 2 == 0
    z_half = red // 2
    sector, member = blk // GROUP, blk % GROUP
    x, y = member // 4, member % 4
    same = x // 2 == z_half
    live = jnp.sum(jnp.where(jnp.arange(occ_live.shape[0]) == sector, occ_live, 0))

    with jax.named_scope("swap"):
        low, high = halves(amplitudes)
        got = between_cores(jnp.where(first, high, low))
        own = jnp.concatenate([jnp.where(first, low, high), got], 1)
        integrals_other = between_cores(integrals)

    with jax.named_scope("line"):
        line_b = hop(own, 12, 3)
        line_a = hop(own, 4, 1)
        line_c = hop(own, 8, 2)
        outer = join(own, line_b)
        inner = join(line_a, line_c)
    with jax.named_scope("plane"):
        a_outer, b_outer = hop(outer, 1, 4), hop(outer, 3, 12)
        a_inner, b_inner = hop(inner, 1, 4), hop(inner, 3, 12)
        c_outer, c_inner = hop(b_outer, 1, 4), hop(a_inner, 3, 12)

    def product(one, two):
        rows = join(one, two)
        dims = (((1,), (1,)), ((), ()))
        total = lax.dot_general(
            rows[:, :cd_dev], integrals, dims, preferred_element_type=jnp.float32
        ) + lax.dot_general(
            rows[:, cd_dev:], integrals_other, dims, preferred_element_type=jnp.float32
        )
        return halves(total)

    pairs = [(outer, inner), (a_outer, b_outer), (a_inner, b_inner), (c_outer, c_inner)]
    with jax.named_scope("products"):
        made = [product(*pair) for pair in pairs]
    (p_outer, p_inner), (pa_outer, pb_outer), (pa_inner, pb_inner), (pc_outer, pc_inner) = made

    mine, away = [], []
    for one, two in made:
        parts = [halves(one), halves(two)]
        mine.append(join(*[jnp.where(same, near, far) for near, far in parts]))
        away.append(join(*[jnp.where(same, far, near) for near, far in parts]))
    near = [p_outer, p_inner, pa_outer, pa_inner]
    far = [pb_outer, pb_inner, pc_outer, pc_inner]

    with jax.named_scope("planes"):
        came = []
        for step in range(5):
            if step == 0:
                load = jnp.where(first, away[0], near[0])
                sends = lambda second, early: not second or early
            elif step < 4:
                load = jnp.where(first, away[step], jnp.where(same, far[step - 1], near[step]))
                sends = lambda second, early: True
            else:
                load = far[3]
                sends = lambda second, early: second and not early
            came.append(between_planes(load, sends))

    with jax.named_scope("finish"):
        done_first = [halves(m + c) for m, c in zip(mine, came[:4])]
        done_second = [
            halves(jnp.where(same, n + c0, f + c1))
            for n, f, c0, c1 in zip(near, far, came[:4], came[1:])
        ]
        (f0p, f0q), (f1p, f1q), (f2p, f2q), (f3p, f3q) = done_first
        (s0p, s0q), (s1p, s1q), (s2p, s2q), (s3p, s3q) = done_second
        one = jnp.where(
            first, jnp.stack([f0p, f1p, f3p, f1q]), jnp.stack([s0p, s1p, s1q, s0q])
        ).astype(jnp.bfloat16)
        two = jnp.where(
            first, jnp.stack([f0q, f2p, f3q, f2q]), jnp.stack([s2p, s3p, s3q, s2q])
        ).astype(jnp.bfloat16)
        column = jnp.where(same, x, x ^ 3)
        keeps_one = (column % 2 == 0) == first
        stay = jnp.where(keeps_one, one, two)
        got = between_cores(jnp.where(keeps_one, two, one))
        rows = jnp.concatenate(
            [jnp.where(first, stay, got), jnp.where(first, got, stay)], 1
        )
        rows = jnp.where(y % 2 == 1, jnp.stack([rows[1], rows[0], rows[3], rows[2]]), rows)
        rows = jnp.where(y // 2 == 1, jnp.stack([rows[2], rows[3], rows[0], rows[1]]), rows)
        rows = rows.reshape(4 * ij_dev, rows.shape[2])
        index = red * rows.shape[0] + jnp.arange(rows.shape[0], dtype=jnp.int32)
        return jnp.where((index < live)[:, None], rows, jnp.zeros((), rows.dtype))


def solution(mesh):
    in_specs = (P("blk", "red"), P("blk", "red"), P())
    out_specs = P("red", "blk")
    return jax.shard_map(
        on_device, mesh=mesh, in_specs=in_specs, out_specs=out_specs, check_vma=False
    )
```

time: 315 us -> 165 us (0.52)
  waiting for transfers between devices: 250 us -> 53.8 us
  starting transfers between devices: 22.7 us -> 81.9 us
  between operations: 13.6 us -> 0.63 us
  matrix products: 15.3 us -> 21.1 us
  other arithmetic: 11.7 us -> 5.94 us
    reduce_scatter x1 -> x0, waiting for transfers between devices: 103 us -> none  [on_device(): lax.psum_scatter(partial_value, 'red', scatter_dimension=0, tiled=True)]
    ppermute x4 -> x17, waiting for transfers between devices: 147 us -> 53.8 us  [the longest x9 31.8 us: hop(): return lax.ppermute(block, AXES, route)]
    ppermute x4 -> x17, starting transfers between devices: 22.7 us -> 81.9 us  [the longest x5 40.9 us: between_planes(): return lax.ppermute(block, AXES, route)]
    select_n x3 -> x10, other arithmetic: 8.54 us -> 2.41 us  [the longest x1 1.07 us: on_device(): own = jnp.concatenate([jnp.where(first, low, high), got], 1)]
    dot_general x5 -> x8, matrix products: 15.3 us -> 21.1 us  [the longest x4 15 us: product(): lax.dot_general(rows[:, cd_dev:], integrals_other, dims, preferred_elemen...]
  transfers between devices with their start and end apart: 5 -> 17, of which waited for: 5 -> 10; matrix products, arithmetic and copies ran while one was open for 4% -> 2% of each run, Pallas kernels for 0% -> 0%
where the time goes in v2:
time: 165 us; the launch traced here: 164 us
  starting transfers between devices  81.9 us (50%)
  waiting for transfers between devices  53.8 us (33%)
  matrix products  21.1 us (13%)
  other arithmetic  5.94 us (4%)
    ppermute x5, starting transfers between devices, between_planes(): return lax.ppermute(block, AXES, route)  40.9 us
    ppermute x9, waiting for transfers between devices, hop(): return lax.ppermute(block, AXES, route)  31.8 us
    ppermute x9, starting transfers between devices, hop(): return lax.ppermute(block, AXES, route)  27.6 us
    ppermute x5, waiting for transfers between devices, between_planes(): return lax.ppermute(block, AXES, route)  20.9 us
    dot_general x4, matrix products, product(): lax.dot_general(rows[:, cd_dev:], integrals_other, dims, preferred_elemen...  15 us
    ppermute x3, starting transfers between devices, between_cores(): lax.ppermute(block, 'red', [(r, r ^ 1) for r in range(lax.axis_size('red'...  13.4 us
    dot_general x4, matrix products, product(): lax.dot_general(rows[:, :cd_dev], integrals, dims, preferred_element_type...  6.12 us
  transfers between devices with their start and end apart: 17, of which 10 were waited for; matrix products, arithmetic and copies ran while one was open for 2% of the time, Pallas kernels for 0%

profile of v2, /device:TPU:1, one launch (start us, length us, event | category | flops | bytes accessed | tf_op | source)
XLA Modules:
  0.0 164.0 jit_solution(16274531128685946363)
XLA Ops:
  1.1 8.8 %collective-permute-start = (bf16[32,4096]{1,0:T(8,128)(2,1)S(1)}, bf16[32,4096]{1,0:T(8,128)(2,1)S(1)}, u32[]{:S(2)}, u32[]{:S(2)}) collective-permute-start(bf16[32,4096]{1,0:T(8,128)(2,1)S(1)} %get-tuple-element.9), channel_id=1, source_target_pairs={{0,1},{1,0},{2,3},{3,2},{4,5},{5,4},{6,7},{7,6},{8,9},{9,8},{10,11... | collective-permute-start | bytes 786440 | tf_op jit(solution)/shard_map/swap/ppermute | solution.py:29
  11.0 1.9 %collective-permute-start.2 = (bf16[32,8192]{1,0:T(8,128)(2,1)S(1)}, bf16[32,8192]{1,0:T(8,128)(2,1)S(1)}, u32[]{:S(2)}, u32[]{:S(2)}) collective-permute-start(bf16[32,8192]{1,0:T(8,128)(2,1)S(1)} %pad_maximum_fusion.2), channel_id=1, source_target_pairs={{0,16},{1,5},{2,18},{3,7},{4,20},{5,1},{6,22},{7,3},{8,24},{9,13},... | collective-permute-start | bytes 1572872 | tf_op jit(solution)/shard_map/line/ppermute | solution.py:25
  13.0 2.3 %collective-permute-start.4 = (bf16[512,4096]{1,0:T(8,128)(2,1)}, bf16[512,4096]{1,0:T(8,128)(2,1)}, u32[]{:S(2)}, u32[]{:S(2)}) collective-permute-start(bf16[512,4096]{1,0:T(8,128)(2,1)} %param.4), channel_id=1, source_target_pairs={{0,1},{1,0},{2,3},{3,2},{4,5},{5,4},{6,7},{7,6},{8,9},{9,8},{10,11... | collective-permute-start | bytes 12582920 | tf_op jit(solution)/shard_map/swap/ppermute | solution.py:29
  15.3 1.9 %collective-permute-start.1 = (bf16[32,8192]{1,0:T(8,128)(2,1)S(1)}, bf16[32,8192]{1,0:T(8,128)(2,1)S(1)}, u32[]{:S(2)}, u32[]{:S(2)}) collective-permute-start(bf16[32,8192]{1,0:T(8,128)(2,1)S(1)} %pad_maximum_fusion.2), channel_id=1, source_target_pairs={{0,48},{1,13},{2,50},{3,15},{4,52},{5,9},{6,54},{7,11},{8,56},{9,5... | collective-permute-start | bytes 1572872 | tf_op jit(solution)/shard_map/line/ppermute | solution.py:25
  17.3 4.8 %collective-permute-start.3 = (bf16[32,8192]{1,0:T(8,128)(2,1)S(1)}, bf16[32,8192]{1,0:T(8,128)(2,1)S(1)}, u32[]{:S(2)}, u32[]{:S(2)}) collective-permute-start(bf16[32,8192]{1,0:T(8,128)(2,1)S(1)} %pad_maximum_fusion.2), channel_id=1, source_target_pairs={{0,32},{1,9},{2,34},{3,11},{4,36},{5,13},{6,38},{7,15},{8,40},{9,1... | collective-permute-start | bytes 1572872 | tf_op jit(solution)/shard_map/line/ppermute | solution.py:25
  22.1 6.9 %collective-permute-done.3 = bf16[32,8192]{1,0:T(8,128)(2,1)S(1)} collective-permute-done((bf16[32,8192]{1,0:T(8,128)(2,1)S(1)}, bf16[32,8192]{1,0:T(8,128)(2,1)S(1)}, u32[]{:S(2)}, u32[]{:S(2)}) %collective-permute-start.3) | collective-permute-done | bytes 524320 | tf_op jit(solution)/shard_map/line/ppermute | solution.py:25
  29.1 3.4 %collective-permute-start.10 = (bf16[64,8192]{1,0:T(8,128)(2,1)S(1)}, bf16[64,8192]{1,0:T(8,128)(2,1)S(1)}, u32[]{:S(2)}, u32[]{:S(2)}) collective-permute-start(bf16[64,8192]{1,0:T(8,128)(2,1)S(1)} %constant_dynamic-update-slice_fusion.2), channel_id=1, source_target_pairs={{0,4},{1,17},{2,6},{3,19},{4,0},{5,21},{6,2},{7,23},{8,12},{9,25},... | collective-permute-start | bytes 3145736 | tf_op jit(solution)/shard_map/plane/ppermute | solution.py:25
  32.6 3.2 %collective-permute-start.6 = (bf16[64,8192]{1,0:T(8,128)(2,1)S(1)}, bf16[64,8192]{1,0:T(8,128)(2,1)S(1)}, u32[]{:S(2)}, u32[]{:S(2)}) collective-permute-start(bf16[64,8192]{1,0:T(8,128)(2,1)S(1)} %pad_maximum_fusion.1), channel_id=1, source_target_pairs={{0,4},{1,17},{2,6},{3,19},{4,0},{5,21},{6,2},{7,23},{8,12},{9,25},... | collective-permute-start | bytes 3145736 | tf_op jit(solution)/shard_map/plane/ppermute | solution.py:25
  35.8 1.9 %collective-permute-start.7 = (bf16[64,8192]{1,0:T(8,128)(2,1)S(1)}, bf16[64,8192]{1,0:T(8,128)(2,1)S(1)}, u32[]{:S(2)}, u32[]{:S(2)}) collective-permute-start(bf16[64,8192]{1,0:T(8,128)(2,1)S(1)} %pad_maximum_fusion.1), channel_id=1, source_target_pairs={{0,12},{1,49},{2,14},{3,51},{4,8},{5,53},{6,10},{7,55},{8,4},{9,57... | collective-permute-start | bytes 3145736 | tf_op jit(solution)/shard_map/plane/ppermute | solution.py:25
  37.7 4.6 %collective-permute-start.12 = (bf16[64,8192]{1,0:T(8,128)(2,1)S(1)}, bf16[64,8192]{1,0:T(8,128)(2,1)S(1)}, u32[]{:S(2)}, u32[]{:S(2)}) collective-permute-start(bf16[64,8192]{1,0:T(8,128)(2,1)S(1)} %constant_dynamic-update-slice_fusion.2), channel_id=1, source_target_pairs={{0,12},{1,49},{2,14},{3,51},{4,8},{5,53},{6,10},{7,55},{8,4},{9,57... | collective-permute-start | bytes 3145736 | tf_op jit(solution)/shard_map/plane/ppermute | solution.py:25
  42.3 1.9 %pad_maximum_fusion = bf16[128,8192]{1,0:T(8,128)(2,1)S(1)} fusion(bf16[32,8192]{1,0:T(8,128)(2,1)S(1)} %collective-permute-done.3, bf16[32,8192]{1,0:T(8,128)(2,1)S(1)} %collective-permute-done.2, bf16[32,8192]{1,0:T(8,128)(2,1)S(1)} %collective-permute-done.1, bf16[32,4096]{1,0:T(8,128)(2,1)S(1)} %collective-permute-done, ...), kind=kLoop, calls=%fused_computation | loop fusion | flops 10485760 | bytes 4194304 | tf_op jit(solution)/shard_map/products/concatenate | solution.py:16
  45.0 2.5 %collective-permute-start.11 = (bf16[64,8192]{1,0:T(8,128)(2,1)S(1)}, bf16[64,8192]{1,0:T(8,128)(2,1)S(1)}, u32[]{:S(2)}, u32[]{:S(2)}) collective-permute-start(bf16[64,8192]{1,0:T(8,128)(2,1)S(1)} %collective-permute-done.10), channel_id=1, source_target_pairs={{0,12},{1,49},{2,14},{3,51},{4,8},{5,53},{6,10},{7,55},{8,4},{9,57... | collective-permute-start | bytes 3145736 | tf_op jit(solution)/shard_map/plane/ppermute | solution.py:25
  47.5 8.7 %collective-permute-done.6 = bf16[64,8192]{1,0:T(8,128)(2,1)S(1)} collective-permute-done((bf16[64,8192]{1,0:T(8,128)(2,1)S(1)}, bf16[64,8192]{1,0:T(8,128)(2,1)S(1)}, u32[]{:S(2)}, u32[]{:S(2)}) %collective-permute-start.6) | collective-permute-done | bytes 1048608 | tf_op jit(solution)/shard_map/plane/ppermute | solution.py:25
  56.3 3.4 %collective-permute-start.9 = (bf16[64,8192]{1,0:T(8,128)(2,1)S(1)}, bf16[64,8192]{1,0:T(8,128)(2,1)S(1)}, u32[]{:S(2)}, u32[]{:S(2)}) collective-permute-start(bf16[64,8192]{1,0:T(8,128)(2,1)S(1)} %collective-permute-done.7), channel_id=1, source_target_pairs={{0,4},{1,17},{2,6},{3,19},{4,0},{5,21},{6,2},{7,23},{8,12},{9,25},... | collective-permute-start | bytes 3145736 | tf_op jit(solution)/shard_map/plane/ppermute | solution.py:25
  59.7 4.4 %collective-permute-done.12 = bf16[64,8192]{1,0:T(8,128)(2,1)S(1)} collective-permute-done((bf16[64,8192]{1,0:T(8,128)(2,1)S(1)}, bf16[64,8192]{1,0:T(8,128)(2,1)S(1)}, u32[]{:S(2)}, u32[]{:S(2)}) %collective-permute-start.12) | collective-permute-done | bytes 1048608 | tf_op jit(solution)/shard_map/plane/ppermute | solution.py:25
  64.2 7.9 %collective-permute-done.9 = bf16[64,8192]{1,0:T(8,128)(2,1)S(1)} collective-permute-done((bf16[64,8192]{1,0:T(8,128)(2,1)S(1)}, bf16[64,8192]{1,0:T(8,128)(2,1)S(1)}, u32[]{:S(2)}, u32[]{:S(2)}) %collective-permute-start.9) | collective-permute-done | bytes 1048608 | tf_op jit(solution)/shard_map/plane/ppermute | solution.py:25
  72.2 3.1 %collective-permute-done.11 = bf16[64,8192]{1,0:T(8,128)(2,1)S(1)} collective-permute-done((bf16[64,8192]{1,0:T(8,128)(2,1)S(1)}, bf16[64,8192]{1,0:T(8,128)(2,1)S(1)}, u32[]{:S(2)}, u32[]{:S(2)}) %collective-permute-start.11) | collective-permute-done | bytes 1048608 | tf_op jit(solution)/shard_map/plane/ppermute | solution.py:25
  75.4 3.9 %fusion.6 = f32[128,512]{1,0:T(8,128)S(1)} fusion(bf16[512,4096]{1,0:T(8,128)(2,1)} %collective-permute-done.4, bf16[128,8192]{1,0:T(8,128)(2,1)S(1)} %constant_dynamic-update-slice_fusion), kind=kOutput, calls=%fused_computation.11 | convolution fusion | flops 536870912 | bytes 5505024 | tf_op jit(solution)/shard_map/products/dot_general | solution.py:75
  79.3 1.5 convolution_add_fusion.2
  80.8 3.7 %fusion.9 = f32[128,512]{1,0:T(8,128)S(1)} fusion(bf16[512,4096]{1,0:T(8,128)(2,1)} %collective-permute-done.4, bf16[128,8192]{1,0:T(8,128)(2,1)S(1)} %pad_maximum_fusion), kind=kOutput, calls=%fused_computation.14 | convolution fusion | flops 536870912 | bytes 5505024 | tf_op jit(solution)/shard_map/products/dot_general | solution.py:75
  84.6 1.5 convolution_add_fusion.3
  86.2 3.7 %fusion = f32[128,512]{1,0:T(8,128)S(1)} fusion(bf16[512,4096]{1,0:T(8,128)(2,1)} %collective-permute-done.4, bf16[128,8192]{1,0:T(8,128)(2,1)S(1)} %constant_dynamic-update-slice_fusion.6), kind=kOutput, calls=%fused_computation.5 | convolution fusion | flops 536870912 | bytes 5505024 | tf_op jit(solution)/shard_map/products/dot_general | solution.py:75
  89.9 1.5 convolution_add_fusion
  91.4 3.7 %fusion.3 = f32[128,512]{1,0:T(8,128)S(1)} fusion(bf16[512,4096]{1,0:T(8,128)(2,1)} %collective-permute-done.4, bf16[128,8192]{1,0:T(8,128)(2,1)S(1)} %constant_dynamic-update-slice_fusion.4), kind=kOutput, calls=%fused_computation.8 | convolution fusion | flops 536870912 | bytes 5505024 | tf_op jit(solution)/shard_map/products/dot_general | solution.py:75
  96.9 12.9 %collective-permute-start.14 = (f32[64,512]{1,0:T(8,128)S(1)}, f32[64,512]{1,0:T(8,128)S(1)}, u32[]{:S(2)}, u32[]{:S(2)}) collective-permute-start(f32[64,512]{1,0:T(8,128)S(1)} %get-tuple-element.28), channel_id=1, source_target_pairs={{0,2},{1,3},{2,0},{3,1},{4,6},{5,7},{6,4},{7,5},{8,10},{9,11},{10,... | collective-permute-start | bytes 393224 | tf_op jit(solution)/shard_map/planes/ppermute | solution.py:40
  109.9 1.9 %collective-permute-start.13 = (f32[64,512]{1,0:T(8,128)S(1)}, f32[64,512]{1,0:T(8,128)S(1)}, u32[]{:S(2)}, u32[]{:S(2)}) collective-permute-start(f32[64,512]{1,0:T(8,128)S(1)} %get-tuple-element.27), channel_id=1, source_target_pairs={{0,2},{1,3},{2,0},{3,1},{4,6},{5,7},{6,4},{7,5},{8,10},{9,11},{10,... | collective-permute-start | bytes 393224 | tf_op jit(solution)/shard_map/planes/ppermute | solution.py:40
  111.8 12.1 %collective-permute-start.15 = (f32[64,512]{1,0:T(8,128)S(1)}, f32[64,512]{1,0:T(8,128)S(1)}, u32[]{:S(2)}, u32[]{:S(2)}) collective-permute-start(f32[64,512]{1,0:T(8,128)S(1)} %get-tuple-element.26), channel_id=1, source_target_pairs={{1,3},{5,7},{9,11},{13,15},{17,19},{21,23},{25,27},{29,31},{35,33}... | collective-permute-start | bytes 393224 | tf_op jit(solution)/shard_map/planes/ppermute | solution.py:40
  125.2 12.7 %collective-permute-start.8 = (f32[64,512]{1,0:T(8,128)S(1)}, f32[64,512]{1,0:T(8,128)S(1)}, u32[]{:S(2)}, u32[]{:S(2)}) collective-permute-start(f32[64,512]{1,0:T(8,128)S(1)} %get-tuple-element.29), channel_id=1, source_target_pairs={{0,2},{1,3},{2,0},{3,1},{4,6},{5,7},{6,4},{7,5},{8,10},{9,11},{10,... | collective-permute-start | bytes 393224 | tf_op jit(solution)/shard_map/planes/ppermute | solution.py:40
  138.0 7.1 %collective-permute-done.15 = f32[64,512]{1,0:T(8,128)S(1)} collective-permute-done((f32[64,512]{1,0:T(8,128)S(1)}, f32[64,512]{1,0:T(8,128)S(1)}, u32[]{:S(2)}, u32[]{:S(2)}) %collective-permute-start.15) | collective-permute-done | bytes 131104 | tf_op jit(solution)/shard_map/planes/ppermute | solution.py:40
  145.1 9.9 %collective-permute-done.5 = f32[64,512]{1,0:T(8,128)S(1)} collective-permute-done((f32[64,512]{1,0:T(8,128)S(1)}, f32[64,512]{1,0:T(8,128)S(1)}, u32[]{:S(2)}, u32[]{:S(2)}) %collective-permute-start.5) | collective-permute-done | bytes 131104 | tf_op jit(solution)/shard_map/planes/ppermute | solution.py:40
  155.1 3.9 %collective-permute-done.8 = f32[64,512]{1,0:T(8,128)S(1)} collective-permute-done((f32[64,512]{1,0:T(8,128)S(1)}, f32[64,512]{1,0:T(8,128)S(1)}, u32[]{:S(2)}, u32[]{:S(2)}) %collective-permute-start.8) | collective-permute-done | bytes 131104 | tf_op jit(solution)/shard_map/planes/ppermute | solution.py:40
  159.3 2.3 %collective-permute-start.16 = (bf16[4,32,512]{2,1,0:T(8,128)(2,1)S(1)}, bf16[4,32,512]{2,1,0:T(8,128)(2,1)S(1)}, u32[]{:S(2)}, u32[]{:S(2)}) collective-permute-start(bf16[4,32,512]{2,1,0:T(8,128)(2,1)S(1)} %get-tuple-element.5), channel_id=1, source_target_pairs={{0,1},{1,0},{2,3},{3,2},{4,5},{5,4},{6,7},{7,6},{8,9},{9,8},{10,11... | collective-permute-start | bytes 393224 | tf_op jit(solution)/shard_map/finish/ppermute | solution.py:29
  (50 shorter events, 9.3 us)
Async XLA Ops:
  1.1 9.9 %collective-permute-start = (bf16[32,4096]{1,0:T(8,128)(2,1)S(1)}, bf16[32,4096]{1,0:T(8,128)(2,1)S(1)}, u32[]{:S(2)}, u32[]{:S(2)}) collective-permute-start(bf16[32,4096]{1,0:T(8,128)(2,1)S(1)} %get-tuple-element.9), channel_id=1, source_target_pairs={{0,1},{1,0},{2,3},{3,2},{4,5},{5,4},{6,7},{7,6},{8,9},{9,8},{10,11... | collective-permute-start | bytes 786440 | tf_op jit(solution)/shard_map/swap/ppermute | solution.py:29
  11.0 11.0 %collective-permute-start.2 = (bf16[32,8192]{1,0:T(8,128)(2,1)S(1)}, bf16[32,8192]{1,0:T(8,128)(2,1)S(1)}, u32[]{:S(2)}, u32[]{:S(2)}) collective-permute-start(bf16[32,8192]{1,0:T(8,128)(2,1)S(1)} %pad_maximum_fusion.2), channel_id=1, source_target_pairs={{0,16},{1,5},{2,18},{3,7},{4,20},{5,1},{6,22},{7,3},{8,24},{9,13},... | collective-permute-start | bytes 1572872 | tf_op jit(solution)/shard_map/line/ppermute | solution.py:25
  13.0 62.4 %collective-permute-start.4 = (bf16[512,4096]{1,0:T(8,128)(2,1)}, bf16[512,4096]{1,0:T(8,128)(2,1)}, u32[]{:S(2)}, u32[]{:S(2)}) collective-permute-start(bf16[512,4096]{1,0:T(8,128)(2,1)} %param.4), channel_id=1, source_target_pairs={{0,1},{1,0},{2,3},{3,2},{4,5},{5,4},{6,7},{7,6},{8,9},{9,8},{10,11... | collective-permute-start | bytes 12582920 | tf_op jit(solution)/shard_map/swap/ppermute | solution.py:29
  15.3 17.2 %collective-permute-start.1 = (bf16[32,8192]{1,0:T(8,128)(2,1)S(1)}, bf16[32,8192]{1,0:T(8,128)(2,1)S(1)}, u32[]{:S(2)}, u32[]{:S(2)}) collective-permute-start(bf16[32,8192]{1,0:T(8,128)(2,1)S(1)} %pad_maximum_fusion.2), channel_id=1, source_target_pairs={{0,48},{1,13},{2,50},{3,15},{4,52},{5,9},{6,54},{7,11},{8,56},{9,5... | collective-permute-start | bytes 1572872 | tf_op jit(solution)/shard_map/line/ppermute | solution.py:25
  17.3 11.8 %collective-permute-start.3 = (bf16[32,8192]{1,0:T(8,128)(2,1)S(1)}, bf16[32,8192]{1,0:T(8,128)(2,1)S(1)}, u32[]{:S(2)}, u32[]{:S(2)}) collective-permute-start(bf16[32,8192]{1,0:T(8,128)(2,1)S(1)} %pad_maximum_fusion.2), channel_id=1, source_target_pairs={{0,32},{1,9},{2,34},{3,11},{4,36},{5,13},{6,38},{7,15},{8,40},{9,1... | collective-permute-start | bytes 1572872 | tf_op jit(solution)/shard_map/line/ppermute | solution.py:25
  29.1 15.9 %collective-permute-start.10 = (bf16[64,8192]{1,0:T(8,128)(2,1)S(1)}, bf16[64,8192]{1,0:T(8,128)(2,1)S(1)}, u32[]{:S(2)}, u32[]{:S(2)}) collective-permute-start(bf16[64,8192]{1,0:T(8,128)(2,1)S(1)} %constant_dynamic-update-slice_fusion.2), channel_id=1, source_target_pairs={{0,4},{1,17},{2,6},{3,19},{4,0},{5,21},{6,2},{7,23},{8,12},{9,25},... | collective-permute-start | bytes 3145736 | tf_op jit(solution)/shard_map/plane/ppermute | solution.py:25
  32.6 23.6 %collective-permute-start.6 = (bf16[64,8192]{1,0:T(8,128)(2,1)S(1)}, bf16[64,8192]{1,0:T(8,128)(2,1)S(1)}, u32[]{:S(2)}, u32[]{:S(2)}) collective-permute-start(bf16[64,8192]{1,0:T(8,128)(2,1)S(1)} %pad_maximum_fusion.1), channel_id=1, source_target_pairs={{0,4},{1,17},{2,6},{3,19},{4,0},{5,21},{6,2},{7,23},{8,12},{9,25},... | collective-permute-start | bytes 3145736 | tf_op jit(solution)/shard_map/plane/ppermute | solution.py:25
  35.8 20.5 %collective-permute-start.7 = (bf16[64,8192]{1,0:T(8,128)(2,1)S(1)}, bf16[64,8192]{1,0:T(8,128)(2,1)S(1)}, u32[]{:S(2)}, u32[]{:S(2)}) collective-permute-start(bf16[64,8192]{1,0:T(8,128)(2,1)S(1)} %pad_maximum_fusion.1), channel_id=1, source_target_pairs={{0,12},{1,49},{2,14},{3,51},{4,8},{5,53},{6,10},{7,55},{8,4},{9,57... | collective-permute-start | bytes 3145736 | tf_op jit(solution)/shard_map/plane/ppermute | solution.py:25
  37.7 26.4 %collective-permute-start.12 = (bf16[64,8192]{1,0:T(8,128)(2,1)S(1)}, bf16[64,8192]{1,0:T(8,128)(2,1)S(1)}, u32[]{:S(2)}, u32[]{:S(2)}) collective-permute-start(bf16[64,8192]{1,0:T(8,128)(2,1)S(1)} %constant_dynamic-update-slice_fusion.2), channel_id=1, source_target_pairs={{0,12},{1,49},{2,14},{3,51},{4,8},{5,53},{6,10},{7,55},{8,4},{9,57... | collective-permute-start | bytes 3145736 | tf_op jit(solution)/shard_map/plane/ppermute | solution.py:25
  45.0 30.3 %collective-permute-start.11 = (bf16[64,8192]{1,0:T(8,128)(2,1)S(1)}, bf16[64,8192]{1,0:T(8,128)(2,1)S(1)}, u32[]{:S(2)}, u32[]{:S(2)}) collective-permute-start(bf16[64,8192]{1,0:T(8,128)(2,1)S(1)} %collective-permute-done.10), channel_id=1, source_target_pairs={{0,12},{1,49},{2,14},{3,51},{4,8},{5,53},{6,10},{7,55},{8,4},{9,57... | collective-permute-start | bytes 3145736 | tf_op jit(solution)/shard_map/plane/ppermute | solution.py:25
  56.3 15.8 %collective-permute-start.9 = (bf16[64,8192]{1,0:T(8,128)(2,1)S(1)}, bf16[64,8192]{1,0:T(8,128)(2,1)S(1)}, u32[]{:S(2)}, u32[]{:S(2)}) collective-permute-start(bf16[64,8192]{1,0:T(8,128)(2,1)S(1)} %collective-permute-done.7), channel_id=1, source_target_pairs={{0,4},{1,17},{2,6},{3,19},{4,0},{5,21},{6,2},{7,23},{8,12},{9,25},... | collective-permute-start | bytes 3145736 | tf_op jit(solution)/shard_map/plane/ppermute | solution.py:25
  75.4 3.9 %copy-start = (bf16[512,4096]{1,0:T(8,128)(2,1)S(1)}, bf16[512,4096]{1,0:T(8,128)(2,1)}, u32[]{:S(2)}) copy-start(bf16[512,4096]{1,0:T(8,128)(2,1)} %param.4) | copy-start | bytes 12582916
  96.9 41.0 %collective-permute-start.14 = (f32[64,512]{1,0:T(8,128)S(1)}, f32[64,512]{1,0:T(8,128)S(1)}, u32[]{:S(2)}, u32[]{:S(2)}) collective-permute-start(f32[64,512]{1,0:T(8,128)S(1)} %get-tuple-element.28), channel_id=1, source_target_pairs={{0,2},{1,3},{2,0},{3,1},{4,6},{5,7},{6,4},{7,5},{8,10},{9,11},{10,... | collective-permute-start | bytes 393224 | tf_op jit(solution)/shard_map/planes/ppermute | solution.py:40
  109.9 28.1 %collective-permute-start.13 = (f32[64,512]{1,0:T(8,128)S(1)}, f32[64,512]{1,0:T(8,128)S(1)}, u32[]{:S(2)}, u32[]{:S(2)}) collective-permute-start(f32[64,512]{1,0:T(8,128)S(1)} %get-tuple-element.27), channel_id=1, source_target_pairs={{0,2},{1,3},{2,0},{3,1},{4,6},{5,7},{6,4},{7,5},{8,10},{9,11},{10,... | collective-permute-start | bytes 393224 | tf_op jit(solution)/shard_map/planes/ppermute | solution.py:40
  111.8 33.3 %collective-permute-start.15 = (f32[64,512]{1,0:T(8,128)S(1)}, f32[64,512]{1,0:T(8,128)S(1)}, u32[]{:S(2)}, u32[]{:S(2)}) collective-permute-start(f32[64,512]{1,0:T(8,128)S(1)} %get-tuple-element.26), channel_id=1, source_target_pairs={{1,3},{5,7},{9,11},{13,15},{17,19},{21,23},{25,27},{29,31},{35,33}... | collective-permute-start | bytes 393224 | tf_op jit(solution)/shard_map/planes/ppermute | solution.py:40
  123.9 31.2 %collective-permute-start.5 = (f32[64,512]{1,0:T(8,128)S(1)}, f32[64,512]{1,0:T(8,128)S(1)}, u32[]{:S(2)}, u32[]{:S(2)}) collective-permute-start(f32[64,512]{1,0:T(8,128)S(1)} %get-tuple-element.30), channel_id=1, source_target_pairs={{0,2},{2,0},{3,1},{4,6},{6,4},{7,5},{8,10},{10,8},{11,9},{12,14},{... | collective-permute-start | bytes 393224 | tf_op jit(solution)/shard_map/planes/ppermute | solution.py:40
  125.2 33.7 %collective-permute-start.8 = (f32[64,512]{1,0:T(8,128)S(1)}, f32[64,512]{1,0:T(8,128)S(1)}, u32[]{:S(2)}, u32[]{:S(2)}) collective-permute-start(f32[64,512]{1,0:T(8,128)S(1)} %get-tuple-element.29), channel_id=1, source_target_pairs={{0,2},{1,3},{2,0},{3,1},{4,6},{5,7},{6,4},{7,5},{8,10},{9,11},{10,... | collective-permute-start | bytes 393224 | tf_op jit(solution)/shard_map/planes/ppermute | solution.py:40
  138.0 23.6 %copy-start.1 = (s32[8]{0:T(128)S(1)}, s32[8]{0:T(128)}, u32[]{:S(2)}) copy-start(s32[8]{0:T(128)} %param.5) | copy-start | bytes 100
  159.3 3.6 %collective-permute-start.16 = (bf16[4,32,512]{2,1,0:T(8,128)(2,1)S(1)}, bf16[4,32,512]{2,1,0:T(8,128)(2,1)S(1)}, u32[]{:S(2)}, u32[]{:S(2)}) collective-permute-start(bf16[4,32,512]{2,1,0:T(8,128)(2,1)S(1)} %get-tuple-element.5), channel_id=1, source_target_pairs={{0,1},{1,0},{2,3},{3,2},{4,5},{5,4},{6,7},{7,6},{8,9},{9,8},{10,11... | collective-permute-start | bytes 393224 | tf_op jit(solution)/shard_map/finish/ppermute | solution.py:29

commit v3 on v1

v3 whole, which is shorter than its diff:
```python
import jax
import jax.numpy as jnp
from jax import lax
from jax.sharding import PartitionSpec as P

GROUP = 16
LANES = 128
STEPS = (60, 32, 16, 8, 4, 2, 1)


def exponents(largest, limit):
    scale = jnp.ones_like(largest)
    exponent = jnp.zeros_like(largest)
    for step in STEPS:
        fits = largest * scale * 2.0**step <= limit
        scale = jnp.where(fits, scale * 2.0**step, scale)
        exponent = jnp.where(fits, exponent + step, exponent)
    return scale, exponent


def unscale(exponent):
    left = exponent.astype(jnp.float32)
    factor = jnp.ones_like(left)
    for step in STEPS:
        taken = left >= step
        factor = jnp.where(taken, factor * 2.0**-step, factor)
        left = jnp.where(taken, left - step, left)
    return factor


def scaled_rows(block):
    wide = block.astype(jnp.float32)
    scale, exponent = exponents(jnp.max(jnp.abs(wide), axis=1, keepdims=True), 32768.0)
    tail = jnp.broadcast_to(exponent, (block.shape[0], LANES))
    return jnp.concatenate([(wide * scale).astype(jnp.float16), tail.astype(jnp.float16)], 1)


def across(block, distance):
    return lax.ppermute(
        block, "red", [(r, r ^ distance) for r in range(lax.axis_size("red"))]
    )


def on_device(amplitudes, integrals, occ_live):
    ij_dev, cd_dev = amplitudes.shape
    n_blk = lax.axis_size("blk")
    planes = [[s * GROUP + m for m in range(GROUP)] for s in range(n_blk // GROUP)]
    blk, red = lax.axis_index("blk"), lax.axis_index("red")
    z_half, core = red // 2, red % 2
    sector = blk // GROUP
    live = jnp.sum(jnp.where(jnp.arange(occ_live.shape[0]) == sector, occ_live, 0))

    gathered = lax.all_gather(
        scaled_rows(amplitudes), "blk", axis_index_groups=planes, axis=0, tiled=True
    )
    product = lax.dot_general(
        gathered[:, :cd_dev].astype(jnp.bfloat16),
        integrals,
        (((1,), (1,)), ((), ())),
        preferred_element_type=jnp.float32,
    )
    product = product * unscale(gathered[:, cd_dev : cd_dev + 1])
    owners = product.reshape(4, 4 * ij_dev, product.shape[1])

    def summed_over_cores(z):
        mine = lax.dynamic_index_in_dim(owners, 2 * z + core, 0, keepdims=False)
        other = lax.dynamic_index_in_dim(owners, 2 * z + 1 - core, 0, keepdims=False)
        return mine + across(other, 1)

    away = summed_over_cores(1 - z_half)
    scale, exponent = exponents(jnp.max(jnp.abs(away), axis=0, keepdims=True), 32767.0)
    tail = jnp.broadcast_to(exponent, (16, away.shape[1]))
    load = jnp.concatenate([jnp.round(away * scale), tail], 0).astype(jnp.int16)
    came = across(load, 2)
    came = came[: away.shape[0]].astype(jnp.float32) * unscale(came[away.shape[0] : away.shape[0] + 1])
    summed = summed_over_cores(z_half) + came
    index = red * summed.shape[0] + jnp.arange(summed.shape[0], dtype=jnp.int32)
    kept = jnp.where((index < live)[:, None], summed, jnp.zeros((), jnp.float32))
    return kept.astype(jnp.bfloat16)


def solution(mesh):
    in_specs = (P("blk", "red"), P("blk", "red"), P())
    out_specs = P("red", "blk")
    return jax.shard_map(
        on_device, mesh=mesh, in_specs=in_specs, out_specs=out_specs, check_vma=False
    )
```

time: 136 us -> 108 us (0.79)
  waiting for transfers between devices: 44.8 us -> 23.6 us
  matrix products: 10.7 us -> 4.53 us
    ppermute x3, waiting for transfers between devices: 44.8 us -> 23.6 us  [across(): lax.ppermute(block, 'red', [(r, r ^ distance) for r in range(lax.axis_siz...]
    dot_general x2 -> x1, matrix products: 10.7 us -> 4.53 us  [on_device(): lax.dot_general(gathered[:, :cd_dev].astype(jnp.bfloat16), integrals, (((...]
  transfers between devices with their start and end apart: 3 -> 3, of which waited for: 1 -> 1; matrix products, arithmetic and copies ran while one was open for 5% -> 1% of each run, Pallas kernels for 0% -> 0%
where the time goes in v3:
time: 108 us
  blocking collectives  53.4 us (49%)
  waiting for transfers between devices  23.6 us (22%)
  starting transfers between devices  19.1 us (18%)
  other arithmetic  5.71 us (5%)
  matrix products  4.53 us (4%)
  local copies, waits for them, and re-layouts  1.16 us (1%)
    all_gather x1, blocking collectives, on_device(): lax.all_gather(scaled_rows(amplitudes), 'blk', axis_index_groups=planes,...  53.4 us
    ppermute x3, waiting for transfers between devices, across(): lax.ppermute(block, 'red', [(r, r ^ distance) for r in range(lax.axis_siz...  23.6 us
    ppermute x3, starting transfers between devices, across(): lax.ppermute(block, 'red', [(r, r ^ distance) for r in range(lax.axis_siz...  19.1 us
    dot_general x1, matrix products, on_device(): lax.dot_general(gathered[:, :cd_dev].astype(jnp.bfloat16), integrals, (((...  4.53 us
  transfers between devices with their start and end apart: 3, of which 1 were waited for; matrix products, arithmetic and copies ran while one was open for 1% of the time, Pallas kernels for 0%

profile of v3, /device:TPU:32, one launch (start us, length us, event | category | flops | bytes accessed | tf_op | source)
XLA Modules:
  0.0 107.7 jit_solution(1302335712281568289)
XLA Ops:
  0.0 1.2 %fusion.2 = f32[64]{0:T(128)S(1)} fusion(bf16[64,4096]{1,0:T(8,128)(2,1)} %param.3), kind=kLoop, calls=%fused_computation.5 | loop fusion | flops 786368 | bytes 524544 | tf_op jit(solution)/shard_map/reduce_max | solution.py:33
  1.3 1.2 %fusion.3 = f16[64,4096]{1,0:T(8,128)(2,1)S(1)} fusion(bf16[64,4096]{1,0:T(8,128)(2,1)} %param.3, f32[64]{0:T(128)S(1)} %get-tuple-element.5), kind=kLoop, calls=%fused_computation.6 | loop fusion | flops 786432 | bytes 1048832 | tf_op jit(solution)/shard_map/convert_element_type | solution.py:35
  2.5 0.1 broadcast_in_dim.38
  2.6 0.1 pad_maximum_fusion
  2.7 0.0 copy-start
  2.7 53.4 %all-gather.1 = f16[1024,4224]{1,0:T(8,128)(2,1)S(1)} all-gather(f16[64,4224]{1,0:T(8,128)(2,1)S(1)} %pad_maximum_fusion), channel_id=1, replica_groups={{0,4,8,12,16,20,24,28,32,36,40,44,48,52,56,60},{64,68,72,76,80,84,88,92..., dimensions={0}, use_global_device_ids=true | all-gather | bytes 9191424 | tf_op jit(solution)/shard_map/all_gather | solution.py:53
  56.1 0.7 fusion.5
  56.8 0.0 copy-done
  56.8 4.5 %fusion.1 = f32[1024,512]{1,0:T(8,128)S(1)} fusion(bf16[512,4096]{1,0:T(8,128)(2,1)S(1)} %copy-done, f16[1024,4224]{1,0:T(8,128)(2,1)S(1)} %all-gather.1, f32[1024]{0:T(1024)S(1)} %fusion.5), kind=kOutput, calls=%fused_computation.2 | convolution fusion | flops 4299685888 | bytes 14684160 | tf_op jit(solution)/shard_map/dot_general | solution.py:56
  61.3 0.0 copy-start.1
  61.4 1.1 dynamic-slice_bitcast_fusion
  62.4 1.9 %collective-permute-start.1 = (f32[256,512]{1,0:T(8,128)}, f32[256,512]{1,0:T(8,128)S(1)}, u32[]{:S(2)}, u32[]{:S(2)}) collective-permute-start(f32[256,512]{1,0:T(8,128)} %get-tuple-element.7), channel_id=1, source_target_pairs={{0,1},{1,0},{2,3},{3,2},{4,5},{5,4},{6,7},{7,6},{8,9},{9,8},{10,11... | collective-permute-start | bytes 1572872 | tf_op jit(solution)/shard_map/ppermute | solution.py:39
  64.3 2.4 %collective-permute-start = (f32[256,512]{1,0:T(8,128)}, f32[256,512]{1,0:T(8,128)S(1)}, u32[]{:S(2)}, u32[]{:S(2)}) collective-permute-start(f32[256,512]{1,0:T(8,128)} %get-tuple-element.8), channel_id=1, source_target_pairs={{0,1},{1,0},{2,3},{3,2},{4,5},{5,4},{6,7},{7,6},{8,9},{9,8},{10,11... | collective-permute-start | bytes 1572872 | tf_op jit(solution)/shard_map/ppermute | solution.py:39
  66.8 0.0 collective-permute-done.1
  66.8 0.1 abs_reduce_fusion
  66.9 0.1 round-nearest-even_convert_fusion
  67.0 14.8 %collective-permute-start.2 = (s16[272,512]{1,0:T(8,128)(2,1)S(1)}, s16[272,512]{1,0:T(8,128)(2,1)S(1)}, u32[]{:S(2)}, u32[]{:S(2)}) collective-permute-start(s16[272,512]{1,0:T(8,128)(2,1)S(1)} %pad_add_fusion), channel_id=1, source_target_pairs={{0,2},{1,3},{2,0},{3,1},{4,6},{5,7},{6,4},{7,5},{8,10},{9,11},{10,... | collective-permute-start | bytes 835592 | tf_op jit(solution)/shard_map/ppermute | solution.py:39
  81.9 0.0 copy-done.1
  81.9 0.6 fusion.12
  82.5 0.7 add_compare_fusion
  83.2 23.6 %collective-permute-done.2 = s16[272,512]{1,0:T(8,128)(2,1)S(1)} collective-permute-done((s16[272,512]{1,0:T(8,128)(2,1)S(1)}, s16[272,512]{1,0:T(8,128)(2,1)S(1)}, u32[]{:S(2)}, u32[]{:S(2)}) %collective-permute-start.2) | collective-permute-done | bytes 278560 | tf_op jit(solution)/shard_map/ppermute | solution.py:39
  106.8 0.0 collective-permute-done
  106.8 0.9 fusion.8
  (6 shorter events, 0.1 us)
Async XLA Ops:
  2.7 54.1 %copy-start = (bf16[512,4096]{1,0:T(8,128)(2,1)S(1)}, bf16[512,4096]{1,0:T(8,128)(2,1)}, u32[]{:S(2)}) copy-start(bf16[512,4096]{1,0:T(8,128)(2,1)} %param.4) | copy-start | bytes 12582916
  61.3 20.6 %copy-start.1 = (s32[8]{0:T(128)S(1)}, s32[8]{0:T(128)}, u32[]{:S(2)}) copy-start(s32[8]{0:T(128)} %param.5) | copy-start | bytes 100
  62.4 4.3 %collective-permute-start.1 = (f32[256,512]{1,0:T(8,128)}, f32[256,512]{1,0:T(8,128)S(1)}, u32[]{:S(2)}, u32[]{:S(2)}) collective-permute-start(f32[256,512]{1,0:T(8,128)} %get-tuple-element.7), channel_id=1, source_target_pairs={{0,1},{1,0},{2,3},{3,2},{4,5},{5,4},{6,7},{7,6},{8,9},{9,8},{10,11... | collective-permute-start | bytes 1572872 | tf_op jit(solution)/shard_map/ppermute | solution.py:39
  64.3 42.5 %collective-permute-start = (f32[256,512]{1,0:T(8,128)}, f32[256,512]{1,0:T(8,128)S(1)}, u32[]{:S(2)}, u32[]{:S(2)}) collective-permute-start(f32[256,512]{1,0:T(8,128)} %get-tuple-element.8), channel_id=1, source_target_pairs={{0,1},{1,0},{2,3},{3,2},{4,5},{5,4},{6,7},{7,6},{8,9},{9,8},{10,11... | collective-permute-start | bytes 1572872 | tf_op jit(solution)/shard_map/ppermute | solution.py:39
  67.0 39.8 %collective-permute-start.2 = (s16[272,512]{1,0:T(8,128)(2,1)S(1)}, s16[272,512]{1,0:T(8,128)(2,1)S(1)}, u32[]{:S(2)}, u32[]{:S(2)}) collective-permute-start(s16[272,512]{1,0:T(8,128)(2,1)S(1)} %pad_add_fusion), channel_id=1, source_target_pairs={{0,2},{1,3},{2,0},{3,1},{4,6},{5,7},{6,4},{7,5},{8,10},{9,11},{10,... | collective-permute-start | bytes 835592 | tf_op jit(solution)/shard_map/ppermute | solution.py:39

commit v4 on v3

--- a/solution.py
+++ b/solution.py
@@ -35,10 +35,10 @@
     return jnp.concatenate([(wide * scale).astype(jnp.float16), tail.astype(jnp.float16)], 1)
 
 
-def across(block, distance):
-    return lax.ppermute(
-        block, "red", [(r, r ^ distance) for r in range(lax.axis_size("red"))]
-    )
+def across(block, distance, pieces=1):
+    route = [(r, r ^ distance) for r in range(lax.axis_size("red"))]
+    moved = [lax.ppermute(piece, "red", route) for piece in jnp.split(block, pieces, 0)]
+    return jnp.concatenate(moved, 0)
 
 
 def on_device(amplitudes, integrals, occ_live):
@@ -60,20 +60,19 @@
         preferred_element_type=jnp.float32,
     )
     product = product * unscale(gathered[:, cd_dev : cd_dev + 1])
-    owners = product.reshape(4, 4 * ij_dev, product.shape[1])
+    owners = [product[4 * ij_dev * r : 4 * ij_dev * (r + 1)] for r in range(4)]
 
-    def summed_over_cores(z):
-        mine = lax.dynamic_index_in_dim(owners, 2 * z + core, 0, keepdims=False)
-        other = lax.dynamic_index_in_dim(owners, 2 * z + 1 - core, 0, keepdims=False)
-        return mine + across(other, 1)
+    def summed_over_cores(low, pieces):
+        even, odd = (jnp.where(low, owners[r], owners[r + 2]) for r in (0, 1))
+        return jnp.where(core == 0, even, odd) + across(jnp.where(core == 0, odd, even), 1, pieces)
 
-    away = summed_over_cores(1 - z_half)
+    away = summed_over_cores(z_half == 1, 1)
     scale, exponent = exponents(jnp.max(jnp.abs(away), axis=0, keepdims=True), 32767.0)
     tail = jnp.broadcast_to(exponent, (16, away.shape[1]))
     load = jnp.concatenate([jnp.round(away * scale), tail], 0).astype(jnp.int16)
     came = across(load, 2)
     came = came[: away.shape[0]].astype(jnp.float32) * unscale(came[away.shape[0] : away.shape[0] + 1])
-    summed = summed_over_cores(z_half) + came
+    summed = summed_over_cores(z_half == 0, 2) + came
     index = red * summed.shape[0] + jnp.arange(summed.shape[0], dtype=jnp.int32)
     kept = jnp.where((index < live)[:, None], summed, jnp.zeros((), jnp.float32))
     return kept.astype(jnp.bfloat16)

time: 108 us -> 107 us (level)
  waiting for transfers between devices: 23.6 us -> 21.2 us
  starting transfers between devices: 19.1 us -> 21.1 us
    ppermute x3 -> x4, waiting for transfers between devices: 23.6 us -> 21.2 us  [across(): lax.ppermute(piece, 'red', route)]
    ppermute x3 -> x4, starting transfers between devices: 19.1 us -> 21.1 us  [across(): lax.ppermute(piece, 'red', route)]
  transfers between devices with their start and end apart: 3 -> 4, of which waited for: 1 -> 2; matrix products, arithmetic and copies ran while one was open for 1% -> 1% of each run, Pallas kernels for 0% -> 0%
where the time goes in v4:
time: 107 us
  blocking collectives  53.4 us (50%)
  waiting for transfers between devices  21.2 us (20%)
  starting transfers between devices  21.1 us (20%)
  other arithmetic  6.04 us (6%)
  matrix products  4.54 us (4%)
    all_gather x1, blocking collectives, on_device(): lax.all_gather(scaled_rows(amplitudes), 'blk', axis_index_groups=planes,...  53.4 us
    ppermute x4, waiting for transfers between devices, across(): lax.ppermute(piece, 'red', route)  21.2 us
    ppermute x4, starting transfers between devices, across(): lax.ppermute(piece, 'red', route)  21.1 us
    dot_general x1, matrix products, on_device(): lax.dot_general(gathered[:, :cd_dev].astype(jnp.bfloat16), integrals, (((...  4.54 us
  transfers between devices with their start and end apart: 4, of which 2 were waited for; matrix products, arithmetic and copies ran while one was open for 1% of the time, Pallas kernels for 0%

profile of v4, /device:TPU:32, one launch (start us, length us, event | category | flops | bytes accessed | tf_op | source)
XLA Modules:
  0.0 106.6 jit_solution(2258141308184606000)
XLA Ops:
  0.0 1.2 %fusion.2 = f32[64]{0:T(128)S(1)} fusion(bf16[64,4096]{1,0:T(8,128)(2,1)} %param.3), kind=kLoop, calls=%fused_computation.5 | loop fusion | flops 786368 | bytes 524544 | tf_op jit(solution)/shard_map/reduce_max | solution.py:33
  1.3 1.2 %fusion.3 = f16[64,4096]{1,0:T(8,128)(2,1)S(1)} fusion(bf16[64,4096]{1,0:T(8,128)(2,1)} %param.3, f32[64]{0:T(128)S(1)} %get-tuple-element.7), kind=kLoop, calls=%fused_computation.6 | loop fusion | flops 786432 | bytes 1048832 | tf_op jit(solution)/shard_map/convert_element_type | solution.py:35
  2.5 0.1 broadcast_in_dim.38
  2.6 0.1 pad_maximum_fusion
  2.7 0.0 copy-start
  2.7 53.4 %all-gather.1 = f16[1024,4224]{1,0:T(8,128)(2,1)S(1)} all-gather(f16[64,4224]{1,0:T(8,128)(2,1)S(1)} %pad_maximum_fusion), channel_id=1, replica_groups={{0,4,8,12,16,20,24,28,32,36,40,44,48,52,56,60},{64,68,72,76,80,84,88,92..., dimensions={0}, use_global_device_ids=true | all-gather | bytes 9191424 | tf_op jit(solution)/shard_map/all_gather | solution.py:53
  56.1 0.7 fusion.5
  56.8 0.0 copy-done
  56.8 0.0 copy-start.1
  56.8 4.5 %fusion.1 = f32[1024,512]{1,0:T(8,128)S(1)} fusion(bf16[512,4096]{1,0:T(8,128)(2,1)S(1)} %copy-done, f16[1024,4224]{1,0:T(8,128)(2,1)S(1)} %all-gather.1, f32[1024]{0:T(1024)S(1)} %fusion.5), kind=kOutput, calls=%fused_computation.2 | convolution fusion | flops 4299685888 | bytes 14684160 | tf_op jit(solution)/shard_map/dot_general | solution.py:56
  61.4 0.2 broadcast_select_fusion
  61.6 1.9 %collective-permute-start.2 = (f32[256,512]{1,0:T(8,128)S(1)}, f32[256,512]{1,0:T(8,128)S(1)}, u32[]{:S(2)}, u32[]{:S(2)}) collective-permute-start(f32[256,512]{1,0:T(8,128)S(1)} %broadcast_select_fusion), channel_id=1, source_target_pairs={{0,1},{1,0},{2,3},{3,2},{4,5},{5,4},{6,7},{7,6},{8,9},{9,8},{10,11... | collective-permute-start | bytes 1572872 | tf_op jit(solution)/shard_map/ppermute | solution.py:40
  63.5 0.0 copy-done.1
  63.5 0.6 fusion.12
  64.2 1.2 %collective-permute-done.2 = f32[256,512]{1,0:T(8,128)S(1)} collective-permute-done((f32[256,512]{1,0:T(8,128)S(1)}, f32[256,512]{1,0:T(8,128)S(1)}, u32[]{:S(2)}, u32[]{:S(2)}) %collective-permute-start.2) | collective-permute-done | bytes 524320 | tf_op jit(solution)/shard_map/ppermute | solution.py:40
  65.4 0.2 abs_reduce_fusion
  65.6 0.1 round-nearest-even_convert_fusion
  65.7 14.8 %collective-permute-start.3 = (s16[272,512]{1,0:T(8,128)(2,1)S(1)}, s16[272,512]{1,0:T(8,128)(2,1)S(1)}, u32[]{:S(2)}, u32[]{:S(2)}) collective-permute-start(s16[272,512]{1,0:T(8,128)(2,1)S(1)} %pad_add_fusion), channel_id=1, source_target_pairs={{0,2},{1,3},{2,0},{3,1},{4,6},{5,7},{6,4},{7,5},{8,10},{9,11},{10,... | collective-permute-start | bytes 835592 | tf_op jit(solution)/shard_map/ppermute | solution.py:40
  80.6 1.9 %collective-permute-start = (f32[128,512]{1,0:T(8,128)S(1)}, f32[128,512]{1,0:T(8,128)S(1)}, u32[]{:S(2)}, u32[]{:S(2)}) collective-permute-start(f32[128,512]{1,0:T(8,128)S(1)} %get-tuple-element.10), channel_id=1, source_target_pairs={{0,1},{1,0},{2,3},{3,2},{4,5},{5,4},{6,7},{7,6},{8,9},{9,8},{10,11... | collective-permute-start | bytes 786440 | tf_op jit(solution)/shard_map/ppermute | solution.py:40
  82.5 2.4 %collective-permute-start.1 = (f32[128,512]{1,0:T(8,128)S(1)}, f32[128,512]{1,0:T(8,128)S(1)}, u32[]{:S(2)}, u32[]{:S(2)}) collective-permute-start(f32[128,512]{1,0:T(8,128)S(1)} %get-tuple-element.11), channel_id=1, source_target_pairs={{0,1},{1,0},{2,3},{3,2},{4,5},{5,4},{6,7},{7,6},{8,9},{9,8},{10,11... | collective-permute-start | bytes 786440 | tf_op jit(solution)/shard_map/ppermute | solution.py:40
  84.9 0.7 add_compare_fusion
  85.6 20.0 %collective-permute-done.3 = s16[272,512]{1,0:T(8,128)(2,1)S(1)} collective-permute-done((s16[272,512]{1,0:T(8,128)(2,1)S(1)}, s16[272,512]{1,0:T(8,128)(2,1)S(1)}, u32[]{:S(2)}, u32[]{:S(2)}) %collective-permute-start.3) | collective-permute-done | bytes 278560 | tf_op jit(solution)/shard_map/ppermute | solution.py:40
  105.6 0.0 collective-permute-done
  105.6 0.0 collective-permute-done.1
  105.6 0.9 fusion.8
  (7 shorter events, 0.2 us)
Async XLA Ops:
  2.7 54.1 %copy-start = (bf16[512,4096]{1,0:T(8,128)(2,1)S(1)}, bf16[512,4096]{1,0:T(8,128)(2,1)}, u32[]{:S(2)}) copy-start(bf16[512,4096]{1,0:T(8,128)(2,1)} %param.4) | copy-start | bytes 12582916
  56.8 6.7 %copy-start.1 = (s32[8]{0:T(128)S(1)}, s32[8]{0:T(128)}, u32[]{:S(2)}) copy-start(s32[8]{0:T(128)} %param.5) | copy-start | bytes 100
  61.6 3.8 %collective-permute-start.2 = (f32[256,512]{1,0:T(8,128)S(1)}, f32[256,512]{1,0:T(8,128)S(1)}, u32[]{:S(2)}, u32[]{:S(2)}) collective-permute-start(f32[256,512]{1,0:T(8,128)S(1)} %broadcast_select_fusion), channel_id=1, source_target_pairs={{0,1},{1,0},{2,3},{3,2},{4,5},{5,4},{6,7},{7,6},{8,9},{9,8},{10,11... | collective-permute-start | bytes 1572872 | tf_op jit(solution)/shard_map/ppermute | solution.py:40
  65.7 39.9 %collective-permute-start.3 = (s16[272,512]{1,0:T(8,128)(2,1)S(1)}, s16[272,512]{1,0:T(8,128)(2,1)S(1)}, u32[]{:S(2)}, u32[]{:S(2)}) collective-permute-start(s16[272,512]{1,0:T(8,128)(2,1)S(1)} %pad_add_fusion), channel_id=1, source_target_pairs={{0,2},{1,3},{2,0},{3,1},{4,6},{5,7},{6,4},{7,5},{8,10},{9,11},{10,... | collective-permute-start | bytes 835592 | tf_op jit(solution)/shard_map/ppermute | solution.py:40
  80.6 25.0 %collective-permute-start = (f32[128,512]{1,0:T(8,128)S(1)}, f32[128,512]{1,0:T(8,128)S(1)}, u32[]{:S(2)}, u32[]{:S(2)}) collective-permute-start(f32[128,512]{1,0:T(8,128)S(1)} %get-tuple-element.10), channel_id=1, source_target_pairs={{0,1},{1,0},{2,3},{3,2},{4,5},{5,4},{6,7},{7,6},{8,9},{9,8},{10,11... | collective-permute-start | bytes 786440 | tf_op jit(solution)/shard_map/ppermute | solution.py:40
  82.5 23.1 %collective-permute-start.1 = (f32[128,512]{1,0:T(8,128)S(1)}, f32[128,512]{1,0:T(8,128)S(1)}, u32[]{:S(2)}, u32[]{:S(2)}) collective-permute-start(f32[128,512]{1,0:T(8,128)S(1)} %get-tuple-element.11), channel_id=1, source_target_pairs={{0,1},{1,0},{2,3},{3,2},{4,5},{5,4},{6,7},{7,6},{8,9},{9,8},{10,11... | collective-permute-start | bytes 786440 | tf_op jit(solution)/shard_map/ppermute | solution.py:40

commit v5 on v4

--- a/solution.py
+++ b/solution.py
@@ -5,6 +5,7 @@
 
 GROUP = 16
 LANES = 128
+RAISE = 12
 STEPS = (60, 32, 16, 8, 4, 2, 1)
 
 
@@ -29,7 +30,8 @@
 
 
 def scaled_rows(block):
-    wide = block.astype(jnp.float32)
+    near = lax.optimization_barrier(block * 2**RAISE)
+    wide = near.astype(jnp.float32)
     scale, exponent = exponents(jnp.max(jnp.abs(wide), axis=1, keepdims=True), 32768.0)
     tail = jnp.broadcast_to(exponent, (block.shape[0], LANES))
     return jnp.concatenate([(wide * scale).astype(jnp.float16), tail.astype(jnp.float16)], 1)
@@ -59,7 +61,7 @@
         (((1,), (1,)), ((), ())),
         preferred_element_type=jnp.float32,
     )
-    product = product * unscale(gathered[:, cd_dev : cd_dev + 1])
+    product = product * 2.0**-RAISE * unscale(gathered[:, cd_dev : cd_dev + 1])
     owners = [product[4 * ij_dev * r : 4 * ij_dev * (r + 1)] for r in range(4)]
 
     def summed_over_cores(low, pieces):
@@ -68,7 +70,7 @@
 
     away = summed_over_cores(z_half == 1, 1)
     scale, exponent = exponents(jnp.max(jnp.abs(away), axis=0, keepdims=True), 32767.0)
-    tail = jnp.broadcast_to(exponent, (16, away.shape[1]))
+    tail = jnp.broadcast_to(exponent, (8, away.shape[1]))
     load = jnp.concatenate([jnp.round(away * scale), tail], 0).astype(jnp.int16)
     came = across(load, 2)
     came = came[: away.shape[0]].astype(jnp.float32) * unscale(came[away.shape[0] : away.shape[0] + 1])

time: 107 us -> 105 us (0.981)
    mul x0 -> x2, other arithmetic: none -> 1.77 us  [the longest x1 1.09 us: scaled_rows(): near = lax.optimization_barrier(block * 2 ** RAISE)]
where the time goes in v5:
time: 105 us
  blocking collectives  53.4 us (51%)
  starting transfers between devices  21.1 us (20%)
  waiting for transfers between devices  20.5 us (20%)
  other arithmetic  5.06 us (5%)
  matrix products  4.54 us (4%)
    all_gather x1, blocking collectives, on_device(): lax.all_gather(scaled_rows(amplitudes), 'blk', axis_index_groups=planes,...  53.4 us
    ppermute x4, starting transfers between devices, across(): lax.ppermute(piece, 'red', route)  21.1 us
    ppermute x4, waiting for transfers between devices, across(): lax.ppermute(piece, 'red', route)  20.5 us
    dot_general x1, matrix products, on_device(): lax.dot_general(gathered[:, :cd_dev].astype(jnp.bfloat16), integrals, (((...  4.54 us
  transfers between devices with their start and end apart: 4, of which 2 were waited for; matrix products, arithmetic and copies ran while one was open for 1% of the time, Pallas kernels for 0%

profile of v5, /device:TPU:32, one launch (start us, length us, event | category | flops | bytes accessed | tf_op | source)
XLA Modules:
  0.0 104.9 jit_solution(12126856771142357932)
XLA Ops:
  0.0 1.1 %broadcast_multiply_fusion = bf16[64,4096]{1,0:T(8,128)(2,1)S(1)} fusion(bf16[64,4096]{1,0:T(8,128)(2,1)} %param.3), kind=kLoop, calls=%fused_computation.36 | loop fusion | flops 262144 | bytes 1048576 | tf_op jit(solution)/shard_map/mul | solution.py:33
  1.1 0.2 fusion.2
  1.3 0.2 fusion.3
  1.5 0.1 broadcast_in_dim.38
  1.6 0.1 pad_maximum_fusion
  1.7 0.0 copy-start
  1.7 53.4 %all-gather.1 = f16[1024,4224]{1,0:T(8,128)(2,1)S(1)} all-gather(f16[64,4224]{1,0:T(8,128)(2,1)S(1)} %pad_maximum_fusion), channel_id=1, replica_groups={{0,4,8,12,16,20,24,28,32,36,40,44,48,52,56,60},{64,68,72,76,80,84,88,92..., dimensions={0}, use_global_device_ids=true | all-gather | bytes 9191424 | tf_op jit(solution)/shard_map/all_gather | solution.py:55
  55.1 0.7 fusion.6
  55.8 0.0 copy-done
  55.8 0.0 copy-start.1
  55.8 4.5 %fusion.1 = f32[1024,512]{1,0:T(8,128)S(1)} fusion(bf16[512,4096]{1,0:T(8,128)(2,1)S(1)} %copy-done, f16[1024,4224]{1,0:T(8,128)(2,1)S(1)} %all-gather.1, f32[1024]{0:T(1024)S(1)} %fusion.6), kind=kOutput, calls=%fused_computation.2 | convolution fusion | flops 4299685888 | bytes 14684160 | tf_op jit(solution)/shard_map/dot_general | solution.py:58
  60.4 0.2 broadcast_select_fusion
  60.6 1.9 %collective-permute-start.2 = (f32[256,512]{1,0:T(8,128)S(1)}, f32[256,512]{1,0:T(8,128)S(1)}, u32[]{:S(2)}, u32[]{:S(2)}) collective-permute-start(f32[256,512]{1,0:T(8,128)S(1)} %broadcast_select_fusion), channel_id=1, source_target_pairs={{0,1},{1,0},{2,3},{3,2},{4,5},{5,4},{6,7},{7,6},{8,9},{9,8},{10,11... | collective-permute-start | bytes 1572872 | tf_op jit(solution)/shard_map/ppermute | solution.py:42
  62.6 0.0 copy-done.1
  62.6 0.6 fusion.13
  63.2 1.2 %collective-permute-done.2 = f32[256,512]{1,0:T(8,128)S(1)} collective-permute-done((f32[256,512]{1,0:T(8,128)S(1)}, f32[256,512]{1,0:T(8,128)S(1)}, u32[]{:S(2)}, u32[]{:S(2)}) %collective-permute-start.2) | collective-permute-done | bytes 524320 | tf_op jit(solution)/shard_map/ppermute | solution.py:42
  64.4 0.2 abs_reduce_fusion
  64.6 0.1 round-nearest-even_convert_fusion
  64.7 14.8 %collective-permute-start.3 = (s16[264,512]{1,0:T(8,128)(2,1)S(1)}, s16[264,512]{1,0:T(8,128)(2,1)S(1)}, u32[]{:S(2)}, u32[]{:S(2)}) collective-permute-start(s16[264,512]{1,0:T(8,128)(2,1)S(1)} %pad_add_fusion), channel_id=1, source_target_pairs={{0,2},{1,3},{2,0},{3,1},{4,6},{5,7},{6,4},{7,5},{8,10},{9,11},{10,... | collective-permute-start | bytes 811016 | tf_op jit(solution)/shard_map/ppermute | solution.py:42
  79.6 1.9 %collective-permute-start = (f32[128,512]{1,0:T(8,128)S(1)}, f32[128,512]{1,0:T(8,128)S(1)}, u32[]{:S(2)}, u32[]{:S(2)}) collective-permute-start(f32[128,512]{1,0:T(8,128)S(1)} %get-tuple-element.10), channel_id=1, source_target_pairs={{0,1},{1,0},{2,3},{3,2},{4,5},{5,4},{6,7},{7,6},{8,9},{9,8},{10,11... | collective-permute-start | bytes 786440 | tf_op jit(solution)/shard_map/ppermute | solution.py:42
  81.5 2.4 %collective-permute-start.1 = (f32[128,512]{1,0:T(8,128)S(1)}, f32[128,512]{1,0:T(8,128)S(1)}, u32[]{:S(2)}, u32[]{:S(2)}) collective-permute-start(f32[128,512]{1,0:T(8,128)S(1)} %get-tuple-element.11), channel_id=1, source_target_pairs={{0,1},{1,0},{2,3},{3,2},{4,5},{5,4},{6,7},{7,6},{8,9},{9,8},{10,11... | collective-permute-start | bytes 786440 | tf_op jit(solution)/shard_map/ppermute | solution.py:42
  83.9 0.7 add_compare_fusion
  84.6 19.3 %collective-permute-done.3 = s16[264,512]{1,0:T(8,128)(2,1)S(1)} collective-permute-done((s16[264,512]{1,0:T(8,128)(2,1)S(1)}, s16[264,512]{1,0:T(8,128)(2,1)S(1)}, u32[]{:S(2)}, u32[]{:S(2)}) %collective-permute-start.3) | collective-permute-done | bytes 270368 | tf_op jit(solution)/shard_map/ppermute | solution.py:42
  103.9 0.0 collective-permute-done
  103.9 0.0 collective-permute-done.1
  104.0 0.9 fusion.9
  (7 shorter events, 0.2 us)
Async XLA Ops:
  1.7 54.1 %copy-start = (bf16[512,4096]{1,0:T(8,128)(2,1)S(1)}, bf16[512,4096]{1,0:T(8,128)(2,1)}, u32[]{:S(2)}) copy-start(bf16[512,4096]{1,0:T(8,128)(2,1)} %param.4) | copy-start | bytes 12582916
  55.8 6.7 %copy-start.1 = (s32[8]{0:T(128)S(1)}, s32[8]{0:T(128)}, u32[]{:S(2)}) copy-start(s32[8]{0:T(128)} %param.5) | copy-start | bytes 100
  60.6 3.8 %collective-permute-start.2 = (f32[256,512]{1,0:T(8,128)S(1)}, f32[256,512]{1,0:T(8,128)S(1)}, u32[]{:S(2)}, u32[]{:S(2)}) collective-permute-start(f32[256,512]{1,0:T(8,128)S(1)} %broadcast_select_fusion), channel_id=1, source_target_pairs={{0,1},{1,0},{2,3},{3,2},{4,5},{5,4},{6,7},{7,6},{8,9},{9,8},{10,11... | collective-permute-start | bytes 1572872 | tf_op jit(solution)/shard_map/ppermute | solution.py:42
  64.7 39.2 %collective-permute-start.3 = (s16[264,512]{1,0:T(8,128)(2,1)S(1)}, s16[264,512]{1,0:T(8,128)(2,1)S(1)}, u32[]{:S(2)}, u32[]{:S(2)}) collective-permute-start(s16[264,512]{1,0:T(8,128)(2,1)S(1)} %pad_add_fusion), channel_id=1, source_target_pairs={{0,2},{1,3},{2,0},{3,1},{4,6},{5,7},{6,4},{7,5},{8,10},{9,11},{10,... | collective-permute-start | bytes 811016 | tf_op jit(solution)/shard_map/ppermute | solution.py:42
  79.6 24.3 %collective-permute-start = (f32[128,512]{1,0:T(8,128)S(1)}, f32[128,512]{1,0:T(8,128)S(1)}, u32[]{:S(2)}, u32[]{:S(2)}) collective-permute-start(f32[128,512]{1,0:T(8,128)S(1)} %get-tuple-element.10), channel_id=1, source_target_pairs={{0,1},{1,0},{2,3},{3,2},{4,5},{5,4},{6,7},{7,6},{8,9},{9,8},{10,11... | collective-permute-start | bytes 786440 | tf_op jit(solution)/shard_map/ppermute | solution.py:42
  81.5 22.4 %collective-permute-start.1 = (f32[128,512]{1,0:T(8,128)S(1)}, f32[128,512]{1,0:T(8,128)S(1)}, u32[]{:S(2)}, u32[]{:S(2)}) collective-permute-start(f32[128,512]{1,0:T(8,128)S(1)} %get-tuple-element.11), channel_id=1, source_target_pairs={{0,1},{1,0},{2,3},{3,2},{4,5},{5,4},{6,7},{7,6},{8,9},{9,8},{10,11... | collective-permute-start | bytes 786440 | tf_op jit(solution)/shard_map/ppermute | solution.py:42

commit v6 on v5

--- a/solution.py
+++ b/solution.py
@@ -68,16 +68,18 @@
         even, odd = (jnp.where(low, owners[r], owners[r + 2]) for r in (0, 1))
         return jnp.where(core == 0, even, odd) + across(jnp.where(core == 0, odd, even), 1, pieces)
 
-    away = summed_over_cores(z_half == 1, 1)
+    def live_rows(block, owner):
+        index = owner * block.shape[0] + jnp.arange(block.shape[0], dtype=jnp.int32)
+        return jnp.where((index < live)[:, None], block, jnp.zeros((), block.dtype))
+
+    away = live_rows(summed_over_cores(z_half == 1, 1), red ^ 2)
     scale, exponent = exponents(jnp.max(jnp.abs(away), axis=0, keepdims=True), 32767.0)
     tail = jnp.broadcast_to(exponent, (8, away.shape[1]))
     load = jnp.concatenate([jnp.round(away * scale), tail], 0).astype(jnp.int16)
     came = across(load, 2)
     came = came[: away.shape[0]].astype(jnp.float32) * unscale(came[away.shape[0] : away.shape[0] + 1])
     summed = summed_over_cores(z_half == 0, 2) + came
-    index = red * summed.shape[0] + jnp.arange(summed.shape[0], dtype=jnp.int32)
-    kept = jnp.where((index < live)[:, None], summed, jnp.zeros((), jnp.float32))
-    return kept.astype(jnp.bfloat16)
+    return live_rows(summed, red).astype(jnp.bfloat16)
 
 
 def solution(mesh):

time: 105 us -> 105 us (level)
  transfers between devices with their start and end apart: 4 -> 4, of which waited for: 2 -> 2; matrix products, arithmetic and copies ran while one was open for 1% -> 2% of each run, Pallas kernels for 0% -> 0%
where the time goes in v6:
time: 105 us
  blocking collectives  53.4 us (51%)
  starting transfers between devices  21.1 us (20%)
  waiting for transfers between devices  19.9 us (19%)
  other arithmetic  5.73 us (5%)
  matrix products  4.54 us (4%)
    all_gather x1, blocking collectives, on_device(): lax.all_gather(scaled_rows(amplitudes), 'blk', axis_index_groups=planes,...  53.4 us
    ppermute x4, starting transfers between devices, across(): lax.ppermute(piece, 'red', route)  21.1 us
    ppermute x4, waiting for transfers between devices, across(): lax.ppermute(piece, 'red', route)  19.9 us
    dot_general x1, matrix products, on_device(): lax.dot_general(gathered[:, :cd_dev].astype(jnp.bfloat16), integrals, (((...  4.54 us
  transfers between devices with their start and end apart: 4, of which 2 were waited for; matrix products, arithmetic and copies ran while one was open for 2% of the time, Pallas kernels for 0%

profile of v6, /device:TPU:32, one launch (start us, length us, event | category | flops | bytes accessed | tf_op | source)
XLA Modules:
  0.0 104.9 jit_solution(13147432246911929521)
XLA Ops:
  0.0 1.1 %broadcast_multiply_fusion = bf16[64,4096]{1,0:T(8,128)(2,1)S(1)} fusion(bf16[64,4096]{1,0:T(8,128)(2,1)} %param.3), kind=kLoop, calls=%fused_computation.36 | loop fusion | flops 262144 | bytes 1048576 | tf_op jit(solution)/shard_map/mul | solution.py:33
  1.1 0.2 fusion.2
  1.3 0.2 fusion.3
  1.5 0.1 broadcast_in_dim.45
  1.6 0.1 pad_maximum_fusion
  1.7 0.0 copy-start
  1.7 53.4 %all-gather.1 = f16[1024,4224]{1,0:T(8,128)(2,1)S(1)} all-gather(f16[64,4224]{1,0:T(8,128)(2,1)S(1)} %pad_maximum_fusion), channel_id=1, replica_groups={{0,4,8,12,16,20,24,28,32,36,40,44,48,52,56,60},{64,68,72,76,80,84,88,92..., dimensions={0}, use_global_device_ids=true | all-gather | bytes 9191424 | tf_op jit(solution)/shard_map/all_gather | solution.py:55
  55.1 0.7 fusion.6
  55.8 0.0 copy-done
  55.8 0.0 copy-start.1
  55.8 4.5 %fusion.1 = f32[1024,512]{1,0:T(8,128)S(1)} fusion(bf16[512,4096]{1,0:T(8,128)(2,1)S(1)} %copy-done, f16[1024,4224]{1,0:T(8,128)(2,1)S(1)} %all-gather.1, f32[1024]{0:T(1024)S(1)} %fusion.6), kind=kOutput, calls=%fused_computation.2 | convolution fusion | flops 4299685888 | bytes 14684160 | tf_op jit(solution)/shard_map/dot_general | solution.py:58
  60.4 0.2 broadcast_select_fusion
  60.6 1.9 %collective-permute-start.2 = (f32[256,512]{1,0:T(8,128)S(1)}, f32[256,512]{1,0:T(8,128)S(1)}, u32[]{:S(2)}, u32[]{:S(2)}) collective-permute-start(f32[256,512]{1,0:T(8,128)S(1)} %broadcast_select_fusion), channel_id=1, source_target_pairs={{0,1},{1,0},{2,3},{3,2},{4,5},{5,4},{6,7},{7,6},{8,9},{9,8},{10,11... | collective-permute-start | bytes 1572872 | tf_op jit(solution)/shard_map/ppermute | solution.py:42
  62.6 0.0 copy-done.1
  62.6 0.6 fusion.13
  63.2 0.7 add_compare_fusion
  63.9 0.6 collective-permute-done.2
  64.4 0.2 abs_reduce_fusion
  64.6 0.1 round-nearest-even_convert_fusion
  64.7 14.8 %collective-permute-start.3 = (s16[264,512]{1,0:T(8,128)(2,1)S(1)}, s16[264,512]{1,0:T(8,128)(2,1)S(1)}, u32[]{:S(2)}, u32[]{:S(2)}) collective-permute-start(s16[264,512]{1,0:T(8,128)(2,1)S(1)} %pad_add_fusion), channel_id=1, source_target_pairs={{0,2},{1,3},{2,0},{3,1},{4,6},{5,7},{6,4},{7,5},{8,10},{9,11},{10,... | collective-permute-start | bytes 811016 | tf_op jit(solution)/shard_map/ppermute | solution.py:42
  79.6 1.9 %collective-permute-start = (f32[128,512]{1,0:T(8,128)S(1)}, f32[128,512]{1,0:T(8,128)S(1)}, u32[]{:S(2)}, u32[]{:S(2)}) collective-permute-start(f32[128,512]{1,0:T(8,128)S(1)} %get-tuple-element.10), channel_id=1, source_target_pairs={{0,1},{1,0},{2,3},{3,2},{4,5},{5,4},{6,7},{7,6},{8,9},{9,8},{10,11... | collective-permute-start | bytes 786440 | tf_op jit(solution)/shard_map/ppermute | solution.py:42
  81.6 2.4 %collective-permute-start.1 = (f32[128,512]{1,0:T(8,128)S(1)}, f32[128,512]{1,0:T(8,128)S(1)}, u32[]{:S(2)}, u32[]{:S(2)}) collective-permute-start(f32[128,512]{1,0:T(8,128)S(1)} %get-tuple-element.11), channel_id=1, source_target_pairs={{0,1},{1,0},{2,3},{3,2},{4,5},{5,4},{6,7},{7,6},{8,9},{9,8},{10,11... | collective-permute-start | bytes 786440 | tf_op jit(solution)/shard_map/ppermute | solution.py:42
  84.0 0.7 add_compare_fusion.1
  84.6 19.3 %collective-permute-done.3 = s16[264,512]{1,0:T(8,128)(2,1)S(1)} collective-permute-done((s16[264,512]{1,0:T(8,128)(2,1)S(1)}, s16[264,512]{1,0:T(8,128)(2,1)S(1)}, u32[]{:S(2)}, u32[]{:S(2)}) %collective-permute-start.3) | collective-permute-done | bytes 270368 | tf_op jit(solution)/shard_map/ppermute | solution.py:42
  104.0 0.0 collective-permute-done
  104.0 0.0 collective-permute-done.1
  104.0 0.9 fusion.9
  (7 shorter events, 0.2 us)
Async XLA Ops:
  1.7 54.1 %copy-start = (bf16[512,4096]{1,0:T(8,128)(2,1)S(1)}, bf16[512,4096]{1,0:T(8,128)(2,1)}, u32[]{:S(2)}) copy-start(bf16[512,4096]{1,0:T(8,128)(2,1)} %param.4) | copy-start | bytes 12582916
  55.8 6.7 %copy-start.1 = (s32[8]{0:T(128)S(1)}, s32[8]{0:T(128)}, u32[]{:S(2)}) copy-start(s32[8]{0:T(128)} %param.5) | copy-start | bytes 100
  60.6 3.8 %collective-permute-start.2 = (f32[256,512]{1,0:T(8,128)S(1)}, f32[256,512]{1,0:T(8,128)S(1)}, u32[]{:S(2)}, u32[]{:S(2)}) collective-permute-start(f32[256,512]{1,0:T(8,128)S(1)} %broadcast_select_fusion), channel_id=1, source_target_pairs={{0,1},{1,0},{2,3},{3,2},{4,5},{5,4},{6,7},{7,6},{8,9},{9,8},{10,11... | collective-permute-start | bytes 1572872 | tf_op jit(solution)/shard_map/ppermute | solution.py:42
  64.7 39.2 %collective-permute-start.3 = (s16[264,512]{1,0:T(8,128)(2,1)S(1)}, s16[264,512]{1,0:T(8,128)(2,1)S(1)}, u32[]{:S(2)}, u32[]{:S(2)}) collective-permute-start(s16[264,512]{1,0:T(8,128)(2,1)S(1)} %pad_add_fusion), channel_id=1, source_target_pairs={{0,2},{1,3},{2,0},{3,1},{4,6},{5,7},{6,4},{7,5},{8,10},{9,11},{10,... | collective-permute-start | bytes 811016 | tf_op jit(solution)/shard_map/ppermute | solution.py:42
  79.6 24.3 %collective-permute-start = (f32[128,512]{1,0:T(8,128)S(1)}, f32[128,512]{1,0:T(8,128)S(1)}, u32[]{:S(2)}, u32[]{:S(2)}) collective-permute-start(f32[128,512]{1,0:T(8,128)S(1)} %get-tuple-element.10), channel_id=1, source_target_pairs={{0,1},{1,0},{2,3},{3,2},{4,5},{5,4},{6,7},{7,6},{8,9},{9,8},{10,11... | collective-permute-start | bytes 786440 | tf_op jit(solution)/shard_map/ppermute | solution.py:42
  81.6 22.4 %collective-permute-start.1 = (f32[128,512]{1,0:T(8,128)S(1)}, f32[128,512]{1,0:T(8,128)S(1)}, u32[]{:S(2)}, u32[]{:S(2)}) collective-permute-start(f32[128,512]{1,0:T(8,128)S(1)} %get-tuple-element.11), channel_id=1, source_target_pairs={{0,1},{1,0},{2,3},{3,2},{4,5},{5,4},{6,7},{7,6},{8,9},{9,8},{10,11... | collective-permute-start | bytes 786440 | tf_op jit(solution)/shard_map/ppermute | solution.py:42

commit v7 on v6

--- a/solution.py
+++ b/solution.py
@@ -7,12 +7,13 @@
 LANES = 128
 RAISE = 12
 STEPS = (60, 32, 16, 8, 4, 2, 1)
+ROW_STEPS = (64, 32, 16, 8, 4)
 
 
-def exponents(largest, limit):
+def exponents(largest, limit, steps=STEPS):
     scale = jnp.ones_like(largest)
     exponent = jnp.zeros_like(largest)
-    for step in STEPS:
+    for step in steps:
         fits = largest * scale * 2.0**step <= limit
         scale = jnp.where(fits, scale * 2.0**step, scale)
         exponent = jnp.where(fits, exponent + step, exponent)
@@ -32,8 +33,10 @@
 def scaled_rows(block):
     near = lax.optimization_barrier(block * 2**RAISE)
     wide = near.astype(jnp.float32)
-    scale, exponent = exponents(jnp.max(jnp.abs(wide), axis=1, keepdims=True), 32768.0)
-    tail = jnp.broadcast_to(exponent, (block.shape[0], LANES))
+    scale, exponent = exponents(jnp.max(jnp.abs(wide), axis=1, keepdims=True), 32768.0, ROW_STEPS)
+    lane = jnp.arange(LANES, dtype=jnp.float32)[None, :]
+    left = exponent - 8.0 * lane
+    tail = jnp.where(left >= 8.0, 2.0**-8, jnp.where(left >= 4.0, 2.0**-4, 1.0))
     return jnp.concatenate([(wide * scale).astype(jnp.float16), tail.astype(jnp.float16)], 1)
 
 
@@ -61,7 +64,7 @@
         (((1,), (1,)), ((), ())),
         preferred_element_type=jnp.float32,
     )
-    product = product * 2.0**-RAISE * unscale(gathered[:, cd_dev : cd_dev + 1])
+    product = product * 2.0**-RAISE * jnp.prod(gathered[:, cd_dev:].astype(jnp.float32), axis=1, keepdims=True)
     owners = [product[4 * ij_dev * r : 4 * ij_dev * (r + 1)] for r in range(4)]
 
     def summed_over_cores(low, pieces):

time: 105 us -> 105 us (level)
  no operation moved by 1% of the time
where the time goes in v7:
time: 105 us; the launch traced here: 104 us
  blocking collectives  53.4 us (51%)
  starting transfers between devices  21.1 us (20%)
  waiting for transfers between devices  19.9 us (19%)
  other arithmetic  5.34 us (5%)
  matrix products  4.54 us (4%)
    all_gather x1, blocking collectives, on_device(): lax.all_gather(scaled_rows(amplitudes), 'blk', axis_index_groups=planes,...  53.4 us
    ppermute x4, starting transfers between devices, across(): lax.ppermute(piece, 'red', route)  21.1 us
    ppermute x4, waiting for transfers between devices, across(): lax.ppermute(piece, 'red', route)  19.9 us
    dot_general x1, matrix products, on_device(): lax.dot_general(gathered[:, :cd_dev].astype(jnp.bfloat16), integrals, (((...  4.54 us
  transfers between devices with their start and end apart: 4, of which 2 were waited for; matrix products, arithmetic and copies ran while one was open for 2% of the time, Pallas kernels for 0%

profile of v7, /device:TPU:32, one launch (start us, length us, event | category | flops | bytes accessed | tf_op | source)
XLA Modules:
  0.0 104.5 jit_solution(1819499912930938044)
XLA Ops:
  0.0 1.1 %broadcast_multiply_fusion = bf16[64,4096]{1,0:T(8,128)(2,1)S(1)} fusion(bf16[64,4096]{1,0:T(8,128)(2,1)} %param.3), kind=kLoop, calls=%fused_computation.21 | loop fusion | flops 262144 | bytes 1048576 | tf_op jit(solution)/shard_map/mul | solution.py:34
  1.1 0.2 fusion.2
  1.3 0.2 fusion.3
  1.5 0.1 select_convert_fusion
  1.6 0.1 pad_maximum_fusion
  1.7 0.0 copy-start
  1.7 53.4 %all-gather.1 = f16[1024,4224]{1,0:T(8,128)(2,1)S(1)} all-gather(f16[64,4224]{1,0:T(8,128)(2,1)S(1)} %pad_maximum_fusion), channel_id=1, replica_groups={{0,4,8,12,16,20,24,28,32,36,40,44,48,52,56,60},{64,68,72,76,80,84,88,92..., dimensions={0}, use_global_device_ids=true | all-gather | bytes 9191424 | tf_op jit(solution)/shard_map/all_gather | solution.py:58
  55.1 0.2 convert_reduce_fusion
  55.4 0.0 copy-done
  55.4 0.0 copy-start.1
  55.4 4.5 %fusion.1 = f32[1024,512]{1,0:T(8,128)S(1)} fusion(bf16[512,4096]{1,0:T(8,128)(2,1)S(1)} %copy-done, f16[1024,4224]{1,0:T(8,128)(2,1)S(1)} %all-gather.1, f32[1024]{0:T(1024)S(1)} %broadcast_multiply_fusion.1), kind=kOutput, calls=%fused_computation.2 | convolution fusion | flops 4299685888 | bytes 14684160 | tf_op jit(solution)/shard_map/dot_general | solution.py:61
  59.9 0.2 broadcast_select_fusion
  60.1 1.9 %collective-permute-start.2 = (f32[256,512]{1,0:T(8,128)S(1)}, f32[256,512]{1,0:T(8,128)S(1)}, u32[]{:S(2)}, u32[]{:S(2)}) collective-permute-start(f32[256,512]{1,0:T(8,128)S(1)} %broadcast_select_fusion), channel_id=1, source_target_pairs={{0,1},{1,0},{2,3},{3,2},{4,5},{5,4},{6,7},{7,6},{8,9},{9,8},{10,11... | collective-permute-start | bytes 1572872 | tf_op jit(solution)/shard_map/ppermute | solution.py:45
  62.1 0.0 copy-done.1
  62.1 0.6 fusion.10
  62.7 0.7 add_compare_fusion
  63.4 0.6 collective-permute-done.2
  64.0 0.2 abs_reduce_fusion
  64.2 0.1 round-nearest-even_convert_fusion
  64.3 14.8 %collective-permute-start.3 = (s16[264,512]{1,0:T(8,128)(2,1)S(1)}, s16[264,512]{1,0:T(8,128)(2,1)S(1)}, u32[]{:S(2)}, u32[]{:S(2)}) collective-permute-start(s16[264,512]{1,0:T(8,128)(2,1)S(1)} %pad_add_fusion), channel_id=1, source_target_pairs={{0,2},{1,3},{2,0},{3,1},{4,6},{5,7},{6,4},{7,5},{8,10},{9,11},{10,... | collective-permute-start | bytes 811016 | tf_op jit(solution)/shard_map/ppermute | solution.py:45
  79.2 1.9 %collective-permute-start = (f32[128,512]{1,0:T(8,128)S(1)}, f32[128,512]{1,0:T(8,128)S(1)}, u32[]{:S(2)}, u32[]{:S(2)}) collective-permute-start(f32[128,512]{1,0:T(8,128)S(1)} %get-tuple-element.10), channel_id=1, source_target_pairs={{0,1},{1,0},{2,3},{3,2},{4,5},{5,4},{6,7},{7,6},{8,9},{9,8},{10,11... | collective-permute-start | bytes 786440 | tf_op jit(solution)/shard_map/ppermute | solution.py:45
  81.1 2.4 %collective-permute-start.1 = (f32[128,512]{1,0:T(8,128)S(1)}, f32[128,512]{1,0:T(8,128)S(1)}, u32[]{:S(2)}, u32[]{:S(2)}) collective-permute-start(f32[128,512]{1,0:T(8,128)S(1)} %get-tuple-element.11), channel_id=1, source_target_pairs={{0,1},{1,0},{2,3},{3,2},{4,5},{5,4},{6,7},{7,6},{8,9},{9,8},{10,11... | collective-permute-start | bytes 786440 | tf_op jit(solution)/shard_map/ppermute | solution.py:45
  83.5 0.7 add_compare_fusion.1
  84.2 19.3 %collective-permute-done.3 = s16[264,512]{1,0:T(8,128)(2,1)S(1)} collective-permute-done((s16[264,512]{1,0:T(8,128)(2,1)S(1)}, s16[264,512]{1,0:T(8,128)(2,1)S(1)}, u32[]{:S(2)}, u32[]{:S(2)}) %collective-permute-start.3) | collective-permute-done | bytes 270368 | tf_op jit(solution)/shard_map/ppermute | solution.py:45
  103.5 0.0 collective-permute-done
  103.5 0.0 collective-permute-done.1
  103.5 0.9 fusion.6
  (9 shorter events, 0.2 us)
Async XLA Ops:
  1.7 53.6 %copy-start = (bf16[512,4096]{1,0:T(8,128)(2,1)S(1)}, bf16[512,4096]{1,0:T(8,128)(2,1)}, u32[]{:S(2)}) copy-start(bf16[512,4096]{1,0:T(8,128)(2,1)} %param.4) | copy-start | bytes 12582916
  55.4 6.7 %copy-start.1 = (s32[8]{0:T(128)S(1)}, s32[8]{0:T(128)}, u32[]{:S(2)}) copy-start(s32[8]{0:T(128)} %param.5) | copy-start | bytes 100
  60.1 3.8 %collective-permute-start.2 = (f32[256,512]{1,0:T(8,128)S(1)}, f32[256,512]{1,0:T(8,128)S(1)}, u32[]{:S(2)}, u32[]{:S(2)}) collective-permute-start(f32[256,512]{1,0:T(8,128)S(1)} %broadcast_select_fusion), channel_id=1, source_target_pairs={{0,1},{1,0},{2,3},{3,2},{4,5},{5,4},{6,7},{7,6},{8,9},{9,8},{10,11... | collective-permute-start | bytes 1572872 | tf_op jit(solution)/shard_map/ppermute | solution.py:45
  64.3 39.2 %collective-permute-start.3 = (s16[264,512]{1,0:T(8,128)(2,1)S(1)}, s16[264,512]{1,0:T(8,128)(2,1)S(1)}, u32[]{:S(2)}, u32[]{:S(2)}) collective-permute-start(s16[264,512]{1,0:T(8,128)(2,1)S(1)} %pad_add_fusion), channel_id=1, source_target_pairs={{0,2},{1,3},{2,0},{3,1},{4,6},{5,7},{6,4},{7,5},{8,10},{9,11},{10,... | collective-permute-start | bytes 811016 | tf_op jit(solution)/shard_map/ppermute | solution.py:45
  79.2 24.3 %collective-permute-start = (f32[128,512]{1,0:T(8,128)S(1)}, f32[128,512]{1,0:T(8,128)S(1)}, u32[]{:S(2)}, u32[]{:S(2)}) collective-permute-start(f32[128,512]{1,0:T(8,128)S(1)} %get-tuple-element.10), channel_id=1, source_target_pairs={{0,1},{1,0},{2,3},{3,2},{4,5},{5,4},{6,7},{7,6},{8,9},{9,8},{10,11... | collective-permute-start | bytes 786440 | tf_op jit(solution)/shard_map/ppermute | solution.py:45
  81.1 22.4 %collective-permute-start.1 = (f32[128,512]{1,0:T(8,128)S(1)}, f32[128,512]{1,0:T(8,128)S(1)}, u32[]{:S(2)}, u32[]{:S(2)}) collective-permute-start(f32[128,512]{1,0:T(8,128)S(1)} %get-tuple-element.11), channel_id=1, source_target_pairs={{0,1},{1,0},{2,3},{3,2},{4,5},{5,4},{6,7},{7,6},{8,9},{9,8},{10,11... | collective-permute-start | bytes 786440 | tf_op jit(solution)/shard_map/ppermute | solution.py:45

commit v8 on v7

--- a/solution.py
+++ b/solution.py
@@ -21,13 +21,7 @@
 
 
 def unscale(exponent):
-    left = exponent.astype(jnp.float32)
-    factor = jnp.ones_like(left)
-    for step in STEPS:
-        taken = left >= step
-        factor = jnp.where(taken, factor * 2.0**-step, factor)
-        left = jnp.where(taken, left - step, left)
-    return factor
+    return jnp.exp2(-exponent.astype(jnp.float32))
 
 
 def scaled_rows(block):

time: 105 us -> 105 us (level)
  no operation moved by 1% of the time
where the time goes in v8:
time: 105 us; the launch traced here: 104 us
  blocking collectives  53.4 us (51%)
  starting transfers between devices  21.1 us (20%)
  waiting for transfers between devices  19.9 us (19%)
  other arithmetic  5.32 us (5%)
  matrix products  4.54 us (4%)
    all_gather x1, blocking collectives, on_device(): lax.all_gather(scaled_rows(amplitudes), 'blk', axis_index_groups=planes,...  53.4 us
    ppermute x4, starting transfers between devices, across(): lax.ppermute(piece, 'red', route)  21.1 us
    ppermute x4, waiting for transfers between devices, across(): lax.ppermute(piece, 'red', route)  19.9 us
    dot_general x1, matrix products, on_device(): lax.dot_general(gathered[:, :cd_dev].astype(jnp.bfloat16), integrals, (((...  4.54 us
  transfers between devices with their start and end apart: 4, of which 2 were waited for; matrix products, arithmetic and copies ran while one was open for 2% of the time, Pallas kernels for 0%

profile of v8, /device:TPU:32, one launch (start us, length us, event | category | flops | bytes accessed | tf_op | source)
XLA Modules:
  0.0 104.4 jit_solution(5810988951084058998)
XLA Ops:
  0.0 1.1 %broadcast_multiply_fusion = bf16[64,4096]{1,0:T(8,128)(2,1)S(1)} fusion(bf16[64,4096]{1,0:T(8,128)(2,1)} %param.3), kind=kLoop, calls=%fused_computation.21 | loop fusion | flops 262144 | bytes 1048576 | tf_op jit(solution)/shard_map/mul | solution.py:28
  1.1 0.2 fusion.2
  1.3 0.2 fusion.3
  1.5 0.1 select_convert_fusion
  1.6 0.1 pad_maximum_fusion
  1.7 0.0 copy-start
  1.7 53.4 %all-gather.1 = f16[1024,4224]{1,0:T(8,128)(2,1)S(1)} all-gather(f16[64,4224]{1,0:T(8,128)(2,1)S(1)} %pad_maximum_fusion), channel_id=1, replica_groups={{0,4,8,12,16,20,24,28,32,36,40,44,48,52,56,60},{64,68,72,76,80,84,88,92..., dimensions={0}, use_global_device_ids=true | all-gather | bytes 9191424 | tf_op jit(solution)/shard_map/all_gather | solution.py:52
  55.1 0.2 convert_reduce_fusion
  55.4 0.0 copy-done
  55.4 0.0 copy-start.1
  55.4 4.5 %fusion.1 = f32[1024,512]{1,0:T(8,128)S(1)} fusion(bf16[512,4096]{1,0:T(8,128)(2,1)S(1)} %copy-done, f16[1024,4224]{1,0:T(8,128)(2,1)S(1)} %all-gather.1, f32[1024]{0:T(1024)S(1)} %broadcast_multiply_fusion.1), kind=kOutput, calls=%fused_computation.2 | convolution fusion | flops 4299685888 | bytes 14684160 | tf_op jit(solution)/shard_map/dot_general | solution.py:55
  59.9 0.2 broadcast_select_fusion
  60.1 1.9 %collective-permute-start.2 = (f32[256,512]{1,0:T(8,128)S(1)}, f32[256,512]{1,0:T(8,128)S(1)}, u32[]{:S(2)}, u32[]{:S(2)}) collective-permute-start(f32[256,512]{1,0:T(8,128)S(1)} %broadcast_select_fusion), channel_id=1, source_target_pairs={{0,1},{1,0},{2,3},{3,2},{4,5},{5,4},{6,7},{7,6},{8,9},{9,8},{10,11... | collective-permute-start | bytes 1572872 | tf_op jit(solution)/shard_map/ppermute | solution.py:39
  62.1 0.0 copy-done.1
  62.1 0.6 fusion.13
  62.7 0.7 add_compare_fusion
  63.4 0.6 collective-permute-done.2
  64.0 0.2 abs_reduce_fusion
  64.2 0.1 round-nearest-even_convert_fusion
  64.3 14.8 %collective-permute-start.3 = (s16[264,512]{1,0:T(8,128)(2,1)S(1)}, s16[264,512]{1,0:T(8,128)(2,1)S(1)}, u32[]{:S(2)}, u32[]{:S(2)}) collective-permute-start(s16[264,512]{1,0:T(8,128)(2,1)S(1)} %pad_add_fusion), channel_id=1, source_target_pairs={{0,2},{1,3},{2,0},{3,1},{4,6},{5,7},{6,4},{7,5},{8,10},{9,11},{10,... | collective-permute-start | bytes 811016 | tf_op jit(solution)/shard_map/ppermute | solution.py:39
  79.2 1.9 %collective-permute-start = (f32[128,512]{1,0:T(8,128)S(1)}, f32[128,512]{1,0:T(8,128)S(1)}, u32[]{:S(2)}, u32[]{:S(2)}) collective-permute-start(f32[128,512]{1,0:T(8,128)S(1)} %get-tuple-element.10), channel_id=1, source_target_pairs={{0,1},{1,0},{2,3},{3,2},{4,5},{5,4},{6,7},{7,6},{8,9},{9,8},{10,11... | collective-permute-start | bytes 786440 | tf_op jit(solution)/shard_map/ppermute | solution.py:39
  81.1 2.4 %collective-permute-start.1 = (f32[128,512]{1,0:T(8,128)S(1)}, f32[128,512]{1,0:T(8,128)S(1)}, u32[]{:S(2)}, u32[]{:S(2)}) collective-permute-start(f32[128,512]{1,0:T(8,128)S(1)} %get-tuple-element.11), channel_id=1, source_target_pairs={{0,1},{1,0},{2,3},{3,2},{4,5},{5,4},{6,7},{7,6},{8,9},{9,8},{10,11... | collective-permute-start | bytes 786440 | tf_op jit(solution)/shard_map/ppermute | solution.py:39
  83.5 0.7 add_compare_fusion.1
  84.2 19.3 %collective-permute-done.3 = s16[264,512]{1,0:T(8,128)(2,1)S(1)} collective-permute-done((s16[264,512]{1,0:T(8,128)(2,1)S(1)}, s16[264,512]{1,0:T(8,128)(2,1)S(1)}, u32[]{:S(2)}, u32[]{:S(2)}) %collective-permute-start.3) | collective-permute-done | bytes 270368 | tf_op jit(solution)/shard_map/ppermute | solution.py:39
  103.5 0.0 collective-permute-done
  103.5 0.0 collective-permute-done.1
  103.5 0.9 fusion.6
  (9 shorter events, 0.2 us)
Async XLA Ops:
  1.7 53.6 %copy-start = (bf16[512,4096]{1,0:T(8,128)(2,1)S(1)}, bf16[512,4096]{1,0:T(8,128)(2,1)}, u32[]{:S(2)}) copy-start(bf16[512,4096]{1,0:T(8,128)(2,1)} %param.4) | copy-start | bytes 12582916
  55.4 6.7 %copy-start.1 = (s32[8]{0:T(128)S(1)}, s32[8]{0:T(128)}, u32[]{:S(2)}) copy-start(s32[8]{0:T(128)} %param.5) | copy-start | bytes 100
  60.1 3.8 %collective-permute-start.2 = (f32[256,512]{1,0:T(8,128)S(1)}, f32[256,512]{1,0:T(8,128)S(1)}, u32[]{:S(2)}, u32[]{:S(2)}) collective-permute-start(f32[256,512]{1,0:T(8,128)S(1)} %broadcast_select_fusion), channel_id=1, source_target_pairs={{0,1},{1,0},{2,3},{3,2},{4,5},{5,4},{6,7},{7,6},{8,9},{9,8},{10,11... | collective-permute-start | bytes 1572872 | tf_op jit(solution)/shard_map/ppermute | solution.py:39
  64.3 39.2 %collective-permute-start.3 = (s16[264,512]{1,0:T(8,128)(2,1)S(1)}, s16[264,512]{1,0:T(8,128)(2,1)S(1)}, u32[]{:S(2)}, u32[]{:S(2)}) collective-permute-start(s16[264,512]{1,0:T(8,128)(2,1)S(1)} %pad_add_fusion), channel_id=1, source_target_pairs={{0,2},{1,3},{2,0},{3,1},{4,6},{5,7},{6,4},{7,5},{8,10},{9,11},{10,... | collective-permute-start | bytes 811016 | tf_op jit(solution)/shard_map/ppermute | solution.py:39
  79.2 24.3 %collective-permute-start = (f32[128,512]{1,0:T(8,128)S(1)}, f32[128,512]{1,0:T(8,128)S(1)}, u32[]{:S(2)}, u32[]{:S(2)}) collective-permute-start(f32[128,512]{1,0:T(8,128)S(1)} %get-tuple-element.10), channel_id=1, source_target_pairs={{0,1},{1,0},{2,3},{3,2},{4,5},{5,4},{6,7},{7,6},{8,9},{9,8},{10,11... | collective-permute-start | bytes 786440 | tf_op jit(solution)/shard_map/ppermute | solution.py:39
  81.1 22.4 %collective-permute-start.1 = (f32[128,512]{1,0:T(8,128)S(1)}, f32[128,512]{1,0:T(8,128)S(1)}, u32[]{:S(2)}, u32[]{:S(2)}) collective-permute-start(f32[128,512]{1,0:T(8,128)S(1)} %get-tuple-element.11), channel_id=1, source_target_pairs={{0,1},{1,0},{2,3},{3,2},{4,5},{5,4},{6,7},{7,6},{8,9},{9,8},{10,11... | collective-permute-start | bytes 786440 | tf_op jit(solution)/shard_map/ppermute | solution.py:39

commit v9 on v7

--- a/solution.py
+++ b/solution.py
@@ -7,7 +7,7 @@
 LANES = 128
 RAISE = 12
 STEPS = (60, 32, 16, 8, 4, 2, 1)
-ROW_STEPS = (64, 32, 16, 8, 4)
+ROW_STEPS = (48, 32, 16, 8, 4)
 
 
 def exponents(largest, limit, steps=STEPS):
@@ -35,7 +35,7 @@
     wide = near.astype(jnp.float32)
     scale, exponent = exponents(jnp.max(jnp.abs(wide), axis=1, keepdims=True), 32768.0, ROW_STEPS)
     lane = jnp.arange(LANES, dtype=jnp.float32)[None, :]
-    left = exponent - 8.0 * lane
+    left = exponent + RAISE - 8.0 * lane
     tail = jnp.where(left >= 8.0, 2.0**-8, jnp.where(left >= 4.0, 2.0**-4, 1.0))
     return jnp.concatenate([(wide * scale).astype(jnp.float16), tail.astype(jnp.float16)], 1)
 
@@ -64,7 +64,7 @@
         (((1,), (1,)), ((), ())),
         preferred_element_type=jnp.float32,
     )
-    product = product * 2.0**-RAISE * jnp.prod(gathered[:, cd_dev:].astype(jnp.float32), axis=1, keepdims=True)
+    product = product * jnp.prod(gathered[:, cd_dev:].astype(jnp.float32), axis=1, keepdims=True)
     owners = [product[4 * ij_dev * r : 4 * ij_dev * (r + 1)] for r in range(4)]
 
     def summed_over_cores(low, pieces):

time: 105 us -> 105 us (level)
  no operation moved by 1% of the time
where the time goes in v9:
time: 105 us; the launch traced here: 104 us
  blocking collectives  53.4 us (51%)
  starting transfers between devices  21.1 us (20%)
  waiting for transfers between devices  19.9 us (19%)
  other arithmetic  5.33 us (5%)
  matrix products  4.53 us (4%)
    all_gather x1, blocking collectives, on_device(): lax.all_gather(scaled_rows(amplitudes), 'blk', axis_index_groups=planes,...  53.4 us
    ppermute x4, starting transfers between devices, across(): lax.ppermute(piece, 'red', route)  21.1 us
    ppermute x4, waiting for transfers between devices, across(): lax.ppermute(piece, 'red', route)  19.9 us
    dot_general x1, matrix products, on_device(): lax.dot_general(gathered[:, :cd_dev].astype(jnp.bfloat16), integrals, (((...  4.53 us
  transfers between devices with their start and end apart: 4, of which 2 were waited for; matrix products, arithmetic and copies ran while one was open for 2% of the time, Pallas kernels for 0%

profile of v9, /device:TPU:32, one launch (start us, length us, event | category | flops | bytes accessed | tf_op | source)
XLA Modules:
  0.0 104.5 jit_solution(17554536575972783965)
XLA Ops:
  0.0 1.1 %broadcast_multiply_fusion = bf16[64,4096]{1,0:T(8,128)(2,1)S(1)} fusion(bf16[64,4096]{1,0:T(8,128)(2,1)} %param.3), kind=kLoop, calls=%fused_computation.21 | loop fusion | flops 262144 | bytes 1048576 | tf_op jit(solution)/shard_map/mul | solution.py:34
  1.1 0.2 fusion.2
  1.3 0.2 fusion.3
  1.5 0.1 select_convert_fusion
  1.6 0.1 pad_maximum_fusion
  1.7 0.0 copy-start
  1.7 53.4 %all-gather.1 = f16[1024,4224]{1,0:T(8,128)(2,1)S(1)} all-gather(f16[64,4224]{1,0:T(8,128)(2,1)S(1)} %pad_maximum_fusion), channel_id=1, replica_groups={{0,4,8,12,16,20,24,28,32,36,40,44,48,52,56,60},{64,68,72,76,80,84,88,92..., dimensions={0}, use_global_device_ids=true | all-gather | bytes 9191424 | tf_op jit(solution)/shard_map/all_gather | solution.py:58
  55.1 0.2 convert_reduce_fusion
  55.3 0.0 copy-done
  55.4 0.0 copy-start.1
  55.4 4.5 %fusion.1 = f32[1024,512]{1,0:T(8,128)S(1)} fusion(bf16[512,4096]{1,0:T(8,128)(2,1)S(1)} %copy-done, f16[1024,4224]{1,0:T(8,128)(2,1)S(1)} %all-gather.1, f32[1024]{0:T(1024)S(1)} %convert_reduce_fusion), kind=kOutput, calls=%fused_computation.2 | convolution fusion | flops 4299685888 | bytes 14684160 | tf_op jit(solution)/shard_map/dot_general | solution.py:61
  59.9 0.2 broadcast_select_fusion
  60.1 1.9 %collective-permute-start.2 = (f32[256,512]{1,0:T(8,128)S(1)}, f32[256,512]{1,0:T(8,128)S(1)}, u32[]{:S(2)}, u32[]{:S(2)}) collective-permute-start(f32[256,512]{1,0:T(8,128)S(1)} %broadcast_select_fusion), channel_id=1, source_target_pairs={{0,1},{1,0},{2,3},{3,2},{4,5},{5,4},{6,7},{7,6},{8,9},{9,8},{10,11... | collective-permute-start | bytes 1572872 | tf_op jit(solution)/shard_map/ppermute | solution.py:45
  62.1 0.0 copy-done.1
  62.1 0.6 fusion.10
  62.7 0.7 add_compare_fusion
  63.4 0.6 collective-permute-done.2
  63.9 0.2 abs_reduce_fusion
  64.1 0.1 round-nearest-even_convert_fusion
  64.3 14.8 %collective-permute-start.3 = (s16[264,512]{1,0:T(8,128)(2,1)S(1)}, s16[264,512]{1,0:T(8,128)(2,1)S(1)}, u32[]{:S(2)}, u32[]{:S(2)}) collective-permute-start(s16[264,512]{1,0:T(8,128)(2,1)S(1)} %pad_add_fusion), channel_id=1, source_target_pairs={{0,2},{1,3},{2,0},{3,1},{4,6},{5,7},{6,4},{7,5},{8,10},{9,11},{10,... | collective-permute-start | bytes 811016 | tf_op jit(solution)/shard_map/ppermute | solution.py:45
  79.1 1.9 %collective-permute-start = (f32[128,512]{1,0:T(8,128)S(1)}, f32[128,512]{1,0:T(8,128)S(1)}, u32[]{:S(2)}, u32[]{:S(2)}) collective-permute-start(f32[128,512]{1,0:T(8,128)S(1)} %get-tuple-element.10), channel_id=1, source_target_pairs={{0,1},{1,0},{2,3},{3,2},{4,5},{5,4},{6,7},{7,6},{8,9},{9,8},{10,11... | collective-permute-start | bytes 786440 | tf_op jit(solution)/shard_map/ppermute | solution.py:45
  81.1 2.4 %collective-permute-start.1 = (f32[128,512]{1,0:T(8,128)S(1)}, f32[128,512]{1,0:T(8,128)S(1)}, u32[]{:S(2)}, u32[]{:S(2)}) collective-permute-start(f32[128,512]{1,0:T(8,128)S(1)} %get-tuple-element.11), channel_id=1, source_target_pairs={{0,1},{1,0},{2,3},{3,2},{4,5},{5,4},{6,7},{7,6},{8,9},{9,8},{10,11... | collective-permute-start | bytes 786440 | tf_op jit(solution)/shard_map/ppermute | solution.py:45
  83.5 0.7 add_compare_fusion.1
  84.2 19.3 %collective-permute-done.3 = s16[264,512]{1,0:T(8,128)(2,1)S(1)} collective-permute-done((s16[264,512]{1,0:T(8,128)(2,1)S(1)}, s16[264,512]{1,0:T(8,128)(2,1)S(1)}, u32[]{:S(2)}, u32[]{:S(2)}) %collective-permute-start.3) | collective-permute-done | bytes 270368 | tf_op jit(solution)/shard_map/ppermute | solution.py:45
  103.5 0.0 collective-permute-done
  103.5 0.0 collective-permute-done.1
  103.5 0.9 fusion.6
  (8 shorter events, 0.2 us)
Async XLA Ops:
  1.7 53.6 %copy-start = (bf16[512,4096]{1,0:T(8,128)(2,1)S(1)}, bf16[512,4096]{1,0:T(8,128)(2,1)}, u32[]{:S(2)}) copy-start(bf16[512,4096]{1,0:T(8,128)(2,1)} %param.4) | copy-start | bytes 12582916
  55.4 6.7 %copy-start.1 = (s32[8]{0:T(128)S(1)}, s32[8]{0:T(128)}, u32[]{:S(2)}) copy-start(s32[8]{0:T(128)} %param.5) | copy-start | bytes 100
  60.1 3.8 %collective-permute-start.2 = (f32[256,512]{1,0:T(8,128)S(1)}, f32[256,512]{1,0:T(8,128)S(1)}, u32[]{:S(2)}, u32[]{:S(2)}) collective-permute-start(f32[256,512]{1,0:T(8,128)S(1)} %broadcast_select_fusion), channel_id=1, source_target_pairs={{0,1},{1,0},{2,3},{3,2},{4,5},{5,4},{6,7},{7,6},{8,9},{9,8},{10,11... | collective-permute-start | bytes 1572872 | tf_op jit(solution)/shard_map/ppermute | solution.py:45
  64.3 39.2 %collective-permute-start.3 = (s16[264,512]{1,0:T(8,128)(2,1)S(1)}, s16[264,512]{1,0:T(8,128)(2,1)S(1)}, u32[]{:S(2)}, u32[]{:S(2)}) collective-permute-start(s16[264,512]{1,0:T(8,128)(2,1)S(1)} %pad_add_fusion), channel_id=1, source_target_pairs={{0,2},{1,3},{2,0},{3,1},{4,6},{5,7},{6,4},{7,5},{8,10},{9,11},{10,... | collective-permute-start | bytes 811016 | tf_op jit(solution)/shard_map/ppermute | solution.py:45
  79.1 24.4 %collective-permute-start = (f32[128,512]{1,0:T(8,128)S(1)}, f32[128,512]{1,0:T(8,128)S(1)}, u32[]{:S(2)}, u32[]{:S(2)}) collective-permute-start(f32[128,512]{1,0:T(8,128)S(1)} %get-tuple-element.10), channel_id=1, source_target_pairs={{0,1},{1,0},{2,3},{3,2},{4,5},{5,4},{6,7},{7,6},{8,9},{9,8},{10,11... | collective-permute-start | bytes 786440 | tf_op jit(solution)/shard_map/ppermute | solution.py:45
  81.1 22.4 %collective-permute-start.1 = (f32[128,512]{1,0:T(8,128)S(1)}, f32[128,512]{1,0:T(8,128)S(1)}, u32[]{:S(2)}, u32[]{:S(2)}) collective-permute-start(f32[128,512]{1,0:T(8,128)S(1)} %get-tuple-element.11), channel_id=1, source_target_pairs={{0,1},{1,0},{2,3},{3,2},{4,5},{5,4},{6,7},{7,6},{8,9},{9,8},{10,11... | collective-permute-start | bytes 786440 | tf_op jit(solution)/shard_map/ppermute | solution.py:45
